TPU v7x, 32 devices: a whole 2x2x4 slice. The times are simulated.
32 devices in a mesh: lat: 16 (over z, y, x), lon: 2 (over core).
Axes of the slice: x: 2, y: 2, z: 4, core: 2. Of those that a mesh axis runs over, the one named last changes fastest.
Arguments:
- ensemble: float32 [81, 10, 32, 256], P(None, None, 'lat', 'lon'), may hold values from -6 to 6
- obs_values: float32 [3, 512], replicated, may hold values from -8 to 8
- obs_errors: float32 [3, 512], replicated, may hold values from 2 to 20
- obs_device: int32 [3, 512], replicated, may hold values from 0 to 31, as said below
- obs_cell: int32 [3, 512], replicated, may hold values from 0 to 2559
- obs_order: int32 [3, 512], replicated, may hold values from 0 to 511, each once within a row
- coupling: int32 [3, 64, 16, 2], P(None, None, 'lat', 'lon'), may hold values 0 or 1
Outputs:
- analysis: float32 [81, 10, 32, 256], P(None, None, 'lat', 'lon')
Inputs may be any that keep to these rules, and one draw needn't show every extreme that they name: `obs_device`: in every batch each state group holds at most 32 observations, and some group holds exactly 32.
All inputs are finite; a program needn't handle non-finite values. No bound on the sum of `coupling` on one device may be relied on, other than what follows from the above.
Results may differ from a plain program's by a relative error of at most 0.0003.
Values sent between devices are 32-bit elements; how exact they have to be, the bound alone decides.
A program may use at most 64 MiB of HBM per device.

v0:
```python
import jax
import jax.numpy as jnp
from jax import lax
from jax.sharding import PartitionSpec as P

HIGH = lax.Precision.HIGHEST


def block_maps(prior_rows, block_ids, values, errors):
    augmented = prior_rows.shape[0]
    members = augmented - 1
    count_blocks = block_ids.shape[0]
    priors_start = jnp.transpose(prior_rows[:, block_ids], (1, 2, 0))
    value_blocks = values[block_ids]
    error_blocks = errors[block_ids]
    identity = jnp.eye(augmented, dtype=jnp.float32)
    identity_stack = jnp.broadcast_to(identity, (count_blocks, augmented, augmented))

    def assimilate(position, product):
        column = lax.dynamic_index_in_dim(priors_start, position, 1, keepdims=False)
        error_now = lax.dynamic_index_in_dim(error_blocks, position, 1, keepdims=False)
        value_now = lax.dynamic_index_in_dim(value_blocks, position, 1, keepdims=False)
        prior = jnp.einsum("bij,bj->bi", product, column, precision=HIGH)
        perturb = prior[:, 1:]
        spread = jnp.sum(perturb * perturb, axis=1) / (members - 1)
        denominator = spread + error_now
        factor_gain = 1.0 / ((members - 1) * denominator)
        shrink = 1.0 / (1.0 + jnp.sqrt(error_now / denominator))
        innovation = value_now - prior[:, 0]
        row_mix = jnp.einsum("bi,bij->bj", perturb, product[:, 1:, :], precision=HIGH)
        column_mix = jnp.concatenate(
            [(factor_gain * innovation)[:, None], -(shrink * factor_gain)[:, None] * perturb],
            axis=1,
        )
        return product + column_mix[:, :, None] * row_mix[:, None, :]

    return lax.fori_loop(0, block_ids.shape[1], assimilate, identity_stack)


def compose(transforms, coupled_row):
    augmented = transforms.shape[1]
    identity = jnp.eye(augmented, dtype=jnp.float32)
    chosen = jnp.where(coupled_row[:, None, None] > 0, transforms, identity[None])
    while chosen.shape[0] > 1:
        chosen = jnp.einsum("kij,kjl->kil", chosen[1::2], chosen[0::2], precision=HIGH)
    return chosen[0]


def local(ensemble, obs_values, obs_errors, obs_device, obs_cell, obs_order, coupling):
    augmented, levels, rows_dev, cols_dev = ensemble.shape
    members_flat = ensemble.reshape(augmented, levels * rows_dev * cols_dev)
    width_lon = lax.axis_size("lon")
    my_index = lax.axis_index("lat") * width_lon + lax.axis_index("lon")
    nbatch = obs_values.shape[0]
    nblocks = coupling.shape[1]
    nobs = obs_order.shape[1]
    per_block = nobs // nblocks
    coupled = coupling.reshape(nbatch, nblocks)

    def priors(source, batch):
        devices = obs_device[batch]
        columns = source[:, obs_cell[batch]]
        contribution = jnp.where((devices == my_index)[None, :], columns, 0.0)
        return lax.psum(contribution, ("lat", "lon"))

    prior_rows = priors(members_flat, 0)
    for batch in range(nbatch):
        block_ids = obs_order[batch].reshape(nblocks, per_block)
        share = nblocks // width_lon
        my_blocks = lax.dynamic_slice_in_dim(block_ids, lax.axis_index("lon") * share, share, 0)
        partial_maps = block_maps(prior_rows, my_blocks, obs_values[batch], obs_errors[batch])
        transforms = lax.all_gather(partial_maps, "lon", axis=0, tiled=True)
        composite = compose(transforms, coupled[batch])
        members_flat = jnp.dot(composite, members_flat, precision=HIGH)
        if batch + 1 < nbatch:
            prior_rows = priors(members_flat, batch + 1)
    return members_flat.reshape(augmented, levels, rows_dev, cols_dev)


def solution(mesh):
    placed = (P(None, None, "lat", "lon"), P(), P(), P(), P(), P(), P(None, None, "lat", "lon"))
    return jax.shard_map(
        local, mesh=mesh, in_specs=placed, out_specs=P(None, None, "lat", "lon"), check_vma=False
    )
```

profile of v0, /device:TPU:0, one launch (start us, length us, event | category | flops | bytes accessed | tf_op | source)
XLA Modules:
  0.0 594.7 jit_solution(2887324065749566755)
XLA Ops:
  7.4 1.5 copy.70
  11.2 1.9 gather_fusion.2
  13.3 1.9 gather_fusion.3
  15.4 125.2 %all-reduce.4.cloned.1.call-done = f32[81,512]{0,1:T(8,128)} async-done(((f32[81,512]{0,1:T(8,128)}), f32[81,512]{0,1:T(8,128)}) %all-reduce.4.cloned.1.call-update) | async-done | bytes 165904 | tf_op jit(solution)/shard_map/psum | solution.py:64
  140.6 1.7 gather_fusion.1
  142.3 39.1 %while.39 = (s32[]{:T(128)}, f32[32,81,81]{2,1,0:T(8,128)S(1)}, f32[32,8,81]{2,1,0:T(8,128)S(1)}, f32[32,8]{1,0:T(8,128)S(1)}, f32[32,8]{1,0:T(8,128)S(1)}, /*index=5*/s32[]{:T(128)}) while((s32[]{:T(128)}, f32[32,81,81]{2,1,0:T(8,128)S(1)}, f32[32,8,81]{2,1,0:T(8,128)S(1)}, f32[32,8]{1,0:T(8,128)S(1)}, f32[32,8]{1,0:T(8,128)S(1)}, ...), condition=%wide.region_3.4_spmd, body=%wide.region_1.3_spmd.sunk | while | flops 5438242 | bytes 4569677 | solution.py:37
  142.3 2.3 fusion.111
  145.3 1.2 fusion.113
  147.2 2.3 fusion.111
  150.2 1.2 fusion.113
  152.1 2.3 fusion.111
  155.1 1.2 fusion.113
  157.0 2.3 fusion.111
  160.0 1.2 fusion.113
  161.9 2.3 fusion.111
  164.9 1.2 fusion.113
  166.8 2.3 fusion.111
  169.8 1.2 fusion.113
  171.7 2.3 fusion.111
  174.7 1.2 fusion.113
  176.6 2.3 fusion.111
  181.4 1.3 copy.71
  183.4 9.9 %all-gather.4.cloned.1.call-done = f32[64,81,81]{2,0,1:T(8,128)} async-done(((f32[32,81,81]{2,0,1:T(8,128)}), f32[64,81,81]{2,0,1:T(8,128)}) %all-gather.4.cloned.1.call-update) | async-done | bytes 1679632 | tf_op jit(solution)/shard_map/all_gather | solution.py:72
  193.4 3.4 copy_select_fusion.2
  196.7 2.5 fusion.27
  199.2 1.3 fusion.38
  202.2 1.4 fusion.73
  206.3 1.9 gather_fusion.6
  208.3 2.0 gather_fusion.7
  210.4 122.0 %all-reduce.6.cloned.1.call-done = f32[81,512]{0,1:T(8,128)} async-done(((f32[81,512]{0,1:T(8,128)}), f32[81,512]{0,1:T(8,128)}) %all-reduce.6.cloned.1.call-update) | async-done | bytes 165904 | tf_op jit(solution)/shard_map/psum | solution.py:64
  332.4 1.7 gather_fusion.5
  334.1 39.1 %while.40 = (s32[]{:T(128)}, f32[32,81,81]{2,1,0:T(8,128)S(1)}, f32[32,8,81]{2,1,0:T(8,128)S(1)}, f32[32,8]{1,0:T(8,128)S(1)}, f32[32,8]{1,0:T(8,128)S(1)}, /*index=5*/s32[]{:T(128)}) while((s32[]{:T(128)}, f32[32,81,81]{2,1,0:T(8,128)S(1)}, f32[32,8,81]{2,1,0:T(8,128)S(1)}, f32[32,8]{1,0:T(8,128)S(1)}, f32[32,8]{1,0:T(8,128)S(1)}, ...), condition=%wide.region_7.8_spmd, body=%wide.region_5.7_spmd.sunk | while | flops 5438242 | bytes 4569677 | solution.py:37
  334.1 2.3 fusion.118
  339.0 2.3 fusion.118
  343.9 2.3 fusion.118
  348.8 2.3 fusion.118
  353.7 2.3 fusion.118
  358.6 2.3 fusion.118
  363.5 2.3 fusion.118
  368.4 2.3 fusion.118
  373.2 1.3 copy.74
  374.7 10.4 %all-gather.6.cloned.1.call-done = f32[64,81,81]{2,0,1:T(8,128)} async-done(((f32[32,81,81]{2,0,1:T(8,128)}), f32[64,81,81]{2,0,1:T(8,128)}) %all-gather.6.cloned.1.call-update) | async-done | bytes 1679632 | tf_op jit(solution)/shard_map/all_gather | solution.py:72
  385.1 3.4 copy_select_fusion.1
  388.5 2.5 fusion.24
  391.0 1.3 fusion.35
  397.5 1.9 gather_fusion.10
  399.6 2.0 gather_fusion.11
  401.6 122.0 %all-reduce.8.cloned.1.call-done = f32[81,512]{0,1:T(8,128)} async-done(((f32[81,512]{0,1:T(8,128)}), f32[81,512]{0,1:T(8,128)}) %all-reduce.8.cloned.1.call-update) | async-done | bytes 165904 | tf_op jit(solution)/shard_map/psum | solution.py:64
  523.6 1.7 gather_fusion.9
  525.4 39.1 %while.41 = (s32[]{:T(128)}, f32[32,81,81]{2,1,0:T(8,128)S(1)}, f32[32,8,81]{2,1,0:T(8,128)S(1)}, f32[32,8]{1,0:T(8,128)S(1)}, f32[32,8]{1,0:T(8,128)S(1)}, /*index=5*/s32[]{:T(128)}) while((s32[]{:T(128)}, f32[32,81,81]{2,1,0:T(8,128)S(1)}, f32[32,8,81]{2,1,0:T(8,128)S(1)}, f32[32,8]{1,0:T(8,128)S(1)}, f32[32,8]{1,0:T(8,128)S(1)}, ...), condition=%wide.region_11.12_spmd, body=%wide.region_9.11_spmd.sunk | while | flops 5438242 | bytes 4569677 | solution.py:37
  525.4 2.3 fusion.125
  530.3 2.3 fusion.125
  535.2 2.3 fusion.125
  540.1 2.3 fusion.125
  544.9 2.3 fusion.125
  549.8 2.3 fusion.125
  554.7 2.3 fusion.125
  559.6 2.3 fusion.125
  564.5 1.3 copy.77
  566.4 10.0 %all-gather.8.cloned.1.call-done = f32[64,81,81]{2,0,1:T(8,128)} async-done(((f32[32,81,81]{2,0,1:T(8,128)}), f32[64,81,81]{2,0,1:T(8,128)}) %all-gather.8.cloned.1.call-update) | async-done | bytes 1679632 | tf_op jit(solution)/shard_map/all_gather | solution.py:72
  576.4 3.4 copy_select_fusion
  579.8 2.5 fusion.21
  582.3 1.3 fusion.32
  586.1 1.3 copy.80
  (264 shorter events, 68.9 us)
Async XLA Ops:
  6.5 2.4 copy-start.5
  6.5 134.0 %all-reduce.4.cloned.1.call-start = ((), (), s32[]{:S(2)}) async-start(), calls=%async_computation | async-start | bytes 524288 | tf_op jit(solution)/shard_map/psum | solution.py:64
  8.9 2.0 copy-start.2
  8.9 2.3 copy-start.3
  10.9 182.5 %all-gather.4.cloned.1.call-start = ((), (), s32[]{:S(2)}) async-start(), calls=%async_computation.1 | async-start | bytes 3981312 | tf_op jit(solution)/shard_map/all_gather | solution.py:72
  11.2 2.0 copy-start.4
  182.8 0.7 copy-start.6
  182.8 149.6 %all-reduce.6.cloned.1.call-start = ((), (), s32[]{:S(2)}) async-start(), calls=%async_computation.2 | async-start | bytes 524288 | tf_op jit(solution)/shard_map/psum | solution.py:64
  203.7 1.5 copy-start
  206.0 179.1 %all-gather.6.cloned.1.call-start = ((), (), s32[]{:S(2)}) async-start(), calls=%async_computation.3 | async-start | bytes 3981312 | tf_op jit(solution)/shard_map/all_gather | solution.py:72
  374.6 149.0 %all-reduce.8.cloned.1.call-start = ((), (), s32[]{:S(2)}) async-start(), calls=%async_computation.4 | async-start | bytes 524288 | tf_op jit(solution)/shard_map/psum | solution.py:64
  392.3 1.7 copy-start.1
  397.2 179.2 %all-gather.8.cloned.1.call-start = ((), (), s32[]{:S(2)}) async-start(), calls=%async_computation.5 | async-start | bytes 3981312 | tf_op jit(solution)/shard_map/all_gather | solution.py:72
Sparse Core Ops, SparseCore 0:
  12.9 127.6 all-reduce.3
  182.9 10.4 all-gather.3
  206.1 126.1 all-reduce.5
  374.7 10.4 all-gather.5
  397.3 126.2 all-reduce.7
  565.9 10.4 all-gather.7
where the time goes:
time: 599 us; the launch traced here: 595 us
  waiting for transfers between devices  400 us (67%)
  matrix products  104 us (17%)
  other arithmetic  43 us (7%)
  local copies, waits for them, and re-layouts  31.5 us (5%)
  between operations  14.4 us (2%)
    psum x3, waiting for transfers between devices, priors(): return lax.psum(contribution, ('lat', 'lon'))  369 us
    dot_general x24, matrix products, assimilate(): prior = jnp.einsum('bij,bj->bi', product, column, precision=HIGH)  56.2 us
    all_gather x3, waiting for transfers between devices, local(): transforms = lax.all_gather(partial_maps, 'lon', axis=0, tiled=True)  30.4 us
    dot_general x24, matrix products, assimilate(): jnp.einsum('bi,bij->bj', perturb, product[:, 1:, :], precision=HIGH)  28.6 us
    dot_general x18, matrix products, compose(): jnp.einsum('kij,kjl->kil', chosen[1::2], chosen[0::2], precision=HIGH)  16.3 us
    add x24, other arithmetic, assimilate(): return product + column_mix[:, :, None] * row_mix[:, None, :]  16.1 us
  transfers between devices with their start and end apart: 6, of which 6 were waited for; matrix products, arithmetic and copies ran while one was open for 2% of the time, Pallas kernels for 0%

commit v1 on v0

v1 whole, which is shorter than its diff:
```python
import functools
import jax
import jax.numpy as jnp
from jax import lax
from jax.experimental import pallas as pl
from jax.experimental.pallas import tpu as pltpu
from jax.sharding import PartitionSpec as P

MESH = pl.DeviceIdType.MESH
GROUP = 32
LANES = 128
VMEM_LIMIT = 32 * 1024 * 1024


def digits_of(n_lat, n_lon):
    def factors(size):
        out, stride = [], 1
        while size > 1:
            f = 4 if size % 4 == 0 else (2 if size % 2 == 0 else size)
            out.append((stride, f))
            stride, size = stride * f, size // f
        return out
    if (n_lat, n_lon) == (16, 2):
        return [("lat", 4, 4), ("lat", 1, 2), ("lat", 2, 2), ("lon", 1, 2)]
    return [("lon", s, f) for s, f in factors(n_lon)] + [("lat", s, f) for s, f in factors(n_lat)]


def slab_of(device, digits, n_lon):
    place = {"lat": device // n_lon, "lon": device % n_lon}
    slab, weight = 0, 1
    for axis, stride, size in digits:
        slab = slab + (place[axis] // stride) % size * weight
        weight *= size
    return slab


def split2(a):
    hi = a.astype(jnp.bfloat16)
    return hi, (a - hi.astype(jnp.float32)).astype(jnp.bfloat16)


def mm3(a, b, dims=((1,), (0,))):
    ah, al = a if isinstance(a, tuple) else split2(a)
    bh, bl = b if isinstance(b, tuple) else split2(b)
    dot = functools.partial(
        lax.dot_general, dimension_numbers=(dims, ((), ())), preferred_element_type=jnp.float32
    )
    return dot(ah, bh) + (dot(ah, bl) + dot(al, bh))


NT = ((1,), (1,))


def pick_kernel(nbatch, cap, capp, aug, per_member, rows, cells_ref, state_ref, extra_ref, x_ref):
    lane = lax.broadcasted_iota(jnp.int32, (aug, LANES), 1)

    def one(index, acc):
        cell = cells_ref[index]
        slab = state_ref[pl.ds(cell // LANES, aug, stride=per_member), :]
        moved = pltpu.roll(slab, lax.rem(index - cell % LANES + 2 * LANES, LANES), 1)
        return jnp.where(lane == index, moved, acc)

    picked = lax.fori_loop(0, nbatch * capp, one, jnp.zeros((aug, LANES), jnp.float32))
    padded = jnp.concatenate([picked, jnp.zeros((LANES - aug, LANES), jnp.float32)], axis=0)
    turned = jnp.transpose(padded)
    x_ref[0:rows - nbatch * capp, :] = (
        lax.broadcasted_iota(jnp.int32, (rows - nbatch * capp, LANES), 0)
        == lax.broadcasted_iota(jnp.int32, (rows - nbatch * capp, LANES), 1)
    ).astype(jnp.float32)
    x_ref[rows - nbatch * capp:rows, :] = turned[0:nbatch * capp, :] + extra_ref[...]


def exchange_kernel(digits, cap, offset, x_ref, buf_ref, send_sem, recv_sem):
    place = {axis: lax.axis_index(axis) for axis in ("lat", "lon")}
    mine = [lax.rem(place[axis] // stride, size) for axis, stride, size in digits]

    def peer(which, step):
        axis, stride, size = digits[which]
        other = lax.rem(mine[which] + step, size)
        moved = dict(place)
        moved[axis] = place[axis] + (other - mine[which]) * stride
        return (moved["lat"], moved["lon"])

    barrier = pltpu.get_barrier_semaphore()
    count = 0
    for which, (_, _, size) in enumerate(digits):
        for step in range(1, size):
            pl.semaphore_signal(barrier, inc=1, device_id=peer(which, step), device_id_type=MESH)
            count += 1
    own = tuple(mine[::-1])
    buf_ref[own] = x_ref[offset:offset + cap, :]
    pl.semaphore_wait(barrier, count)

    slots = [0]
    sends = []

    def send(part, device):
        slot = slots[0]
        slots[0] += 1
        copy = pltpu.make_async_remote_copy(
            src_ref=buf_ref.at[part], dst_ref=buf_ref.at[part],
            send_sem=send_sem.at[slot], recv_sem=recv_sem.at[slot],
            device_id=device, device_id_type=MESH,
        )
        copy.start()
        sends.append(copy)
        return copy

    if [size for _, _, size in digits] == [4, 2, 2, 2]:
        z, x, y, k = mine
        first = [send((k, y, x, z), peer(0, step)) for step in (1, 2, 3)]
        for copy in first:
            copy.wait_recv()
        to_x = send((k, y, x), peer(1, 1))
        to_y = send((k, y, x), peer(2, 1))
        last = [send((k, y, x), peer(3, 1))]
        to_x.wait_recv()
        diag = [send((k, y, 1 - x, pl.ds(0, 2)), peer(2, 1))]
        to_y.wait_recv()
        diag.append(send((k, 1 - y, x, pl.ds(2, 2)), peer(1, 1)))
        last.append(send((k, y, 1 - x), peer(3, 1)))
        last.append(send((k, 1 - y, x), peer(3, 1)))
        for copy in diag:
            copy.wait_recv()
        last.append(send((k, 1 - y, 1 - x), peer(3, 1)))
        for copy in last:
            copy.wait_recv()
    else:
        for which, (_, _, size) in enumerate(digits):
            part = tuple(mine[which:][::-1])
            stage = [send(part, peer(which, step)) for step in range(1, size)]
            for copy in stage:
                copy.wait_recv()
    for copy in sends:
        copy.wait_send()


def exchange(x, digits, cap, offset, ident):
    shape = tuple(size for _, _, size in digits[::-1]) + (cap, LANES)
    copies = 16 if [s for _, _, s in digits] == [4, 2, 2, 2] else sum(s - 1 for _, _, s in digits)
    return pl.pallas_call(
        functools.partial(exchange_kernel, digits, cap, offset),
        out_shape=jax.ShapeDtypeStruct(shape, jnp.float32),
        in_specs=[pl.BlockSpec(memory_space=pltpu.VMEM)],
        out_specs=pl.BlockSpec(memory_space=pltpu.VMEM),
        scratch_shapes=[pltpu.SemaphoreType.DMA((copies,)), pltpu.SemaphoreType.DMA((copies,))],
        compiler_params=pltpu.CompilerParams(
            collective_id=ident, has_side_effects=True, vmem_limit_bytes=VMEM_LIMIT
        ),
        name="exchange",
    )(x)


def group_update(z, valid, x, per_block, members):
    lane = lax.broadcasted_iota(jnp.int32, (GROUP, LANES), 1)
    is_member = (lane >= 1) & (lane <= members)
    z = list(z)
    hs, vs, ws = [], [], []
    for i in range(per_block):
        p = z[i]
        h = jnp.where(is_member, p, 0.0)
        s = jnp.sum(h * h, axis=1, keepdims=True) / (members - 1)
        y = p[:, members + 1:members + 2]
        r = p[:, members + 2:members + 3]
        q = s + r
        c = 1.0 / ((members - 1) * q)
        a = 1.0 / (1.0 + jnp.sqrt(r / q))
        d = y - p[:, 0:1]
        v = jnp.where(lane == 0, c * d, -(a * c) * h)
        for j in range(i + 1, per_block):
            z[j] = z[j] + v * jnp.sum(h * z[j], axis=1, keepdims=True)
        w = h
        for j in range(i):
            w = w + ws[j] * jnp.sum(h * vs[j], axis=1, keepdims=True)
        vs.append(v)
        ws.append(w)
    v_all = split2(jnp.concatenate([v * valid for v in vs], axis=0))
    w_all = split2(jnp.concatenate(ws, axis=0))
    size = per_block * GROUP
    upper = mm3(v_all, w_all, NT)
    row = lax.broadcasted_iota(jnp.int32, (size, size), 0) & (GROUP - 1)
    col = lax.broadcasted_iota(jnp.int32, (size, size), 1) & (GROUP - 1)
    differ = row ^ col
    levels = GROUP.bit_length() - 1
    ahead = row < col
    inverse = jnp.where(
        lax.broadcasted_iota(jnp.int32, (size, size), 0)
        == lax.broadcasted_iota(jnp.int32, (size, size), 1), 1.0,
        jnp.where(ahead & (differ == 1), upper, 0.0),
    )
    for level in range(1, levels):
        pairs = ahead & (differ >= (1 << level)) & (differ < (2 << level))
        parts = split2(inverse)
        inverse = inverse + mm3(mm3(parts, jnp.where(pairs, upper, 0.0)), parts)
    return x + mm3(mm3(mm3(x, w_all, NT), inverse), v_all)


def update_kernel(batch, per_block, members, count_ref, list_ref, pos_ref, x_ref, buf_ref, out_ref, z_ref):
    out_ref[...] = x_ref[...]
    total = count_ref[batch]

    @pl.loop(0, (total + GROUP - 1) // GROUP)
    def _(group):
        start = group * GROUP

        @pl.loop(0, GROUP)
        def _(b):
            block = list_ref[batch, start + b]
            for i in range(per_block):
                source = pos_ref[batch, block * per_block + i]
                z_ref[pl.ds(i * GROUP + b, 1), :] = buf_ref[pl.ds(source, 1), :]

        valid = (
            start + lax.broadcasted_iota(jnp.int32, (GROUP, 1), 0) < total
        ).astype(jnp.float32)
        z = [z_ref[i * GROUP:(i + 1) * GROUP, :] for i in range(per_block)]
        out_ref[...] = group_update(z, valid, out_ref[...], per_block, members)


def final_kernel(aug, per_member, x_ref, state_ref, out_ref):
    turned = jnp.transpose(x_ref[0:LANES, :])
    parts = split2(turned[0:aug, 0:aug])
    for j in range(0, per_member, 2):
        cut = [state_ref[pl.ds(j + k, aug, stride=per_member), :] for k in range(2)]
        new = mm3(parts, jnp.concatenate(cut, axis=1))
        for k in range(2):
            out_ref[pl.ds(j + k, aug, stride=per_member), :] = new[:, k * LANES:(k + 1) * LANES]


def vspec():
    return pl.BlockSpec(memory_space=pltpu.VMEM)


def sspec():
    return pl.BlockSpec(memory_space=pltpu.SMEM)


def local(ensemble, obs_values, obs_errors, obs_device, obs_cell, obs_order, coupling):
    aug, levels, rows_dev, cols_dev = ensemble.shape
    members = aug - 1
    n_lat, n_lon = lax.axis_size("lat"), lax.axis_size("lon")
    ndev = n_lat * n_lon
    nbatch, nobs = obs_values.shape
    nblocks = coupling.shape[1]
    per_block = nobs // nblocks
    cap = max(1, 2 * nobs // ndev)
    capp = -(-cap // 8) * 8
    digits = digits_of(n_lat, n_lon)
    me = lax.axis_index("lat") * n_lon + lax.axis_index("lon")
    per_member = levels * rows_dev * cols_dev // LANES
    state = ensemble.reshape(aug * per_member, LANES)
    params = pltpu.CompilerParams(vmem_limit_bytes=VMEM_LIMIT)

    same = obs_device[:, :, None] == obs_device[:, None, :]
    before = lax.iota(jnp.int32, nobs)[None, :] < lax.iota(jnp.int32, nobs)[:, None]
    rank = jnp.sum((same & before[None]).astype(jnp.int32), axis=2)
    pos = slab_of(obs_device, digits, n_lon) * cap + rank
    pos_sorted = jnp.take_along_axis(pos, obs_order, axis=1)
    slots = lax.iota(jnp.int32, capp)
    chosen = (obs_device == me)[:, None, :] & (rank[:, None, :] == slots[None, :, None])
    cells = jnp.sum(jnp.where(chosen, obs_cell[:, None, :], 0), axis=2).reshape(nbatch * capp)
    value_own = jnp.sum(jnp.where(chosen, obs_values[:, None, :], 0.0), axis=2).reshape(nbatch * capp, 1)
    error_own = jnp.sum(jnp.where(chosen, obs_errors[:, None, :], 0.0), axis=2).reshape(nbatch * capp, 1)
    lanes = lax.iota(jnp.int32, LANES)[None, :]
    extra = jnp.where(lanes == aug, value_own, jnp.where(lanes == aug + 1, error_own, 0.0))

    coupled = coupling.reshape(nbatch, nblocks) > 0
    blocks = lax.iota(jnp.int32, nblocks)
    earlier = jnp.sum((coupled[:, None, :] & (blocks[None, :] < blocks[:, None])[None]).astype(jnp.int32), axis=2)
    count = jnp.sum(coupled.astype(jnp.int32), axis=1)
    hit = coupled[:, None, :] & (earlier[:, None, :] == blocks[None, :, None])
    listed = jnp.sum(jnp.where(hit, blocks[None, None, :], 0), axis=2)
    if nblocks % GROUP:
        listed = jnp.pad(listed, ((0, 0), (0, GROUP - nblocks % GROUP)))

    base = LANES
    rows = base + nbatch * capp
    x = pl.pallas_call(
        functools.partial(pick_kernel, nbatch, cap, capp, aug, per_member, rows),
        out_shape=jax.ShapeDtypeStruct((rows, LANES), jnp.float32),
        in_specs=[sspec(), vspec(), vspec()],
        out_specs=vspec(),
        compiler_params=params,
        name="pick",
    )(cells, state, extra)

    for batch in range(nbatch):
        buf = exchange(x, digits, cap, base + batch * capp, batch)
        x = pl.pallas_call(
            functools.partial(update_kernel, batch, per_block, members),
            out_shape=jax.ShapeDtypeStruct((rows, LANES), jnp.float32),
            in_specs=[sspec(), sspec(), sspec(), vspec(), vspec()],
            out_specs=vspec(),
            scratch_shapes=[pltpu.VMEM((per_block * GROUP, LANES), jnp.float32)],
            compiler_params=params,
            name="update",
        )(count, listed, pos_sorted, x, buf.reshape(ndev * cap, LANES))

    out = pl.pallas_call(
        functools.partial(final_kernel, aug, per_member),
        out_shape=jax.ShapeDtypeStruct((aug * per_member, LANES), jnp.float32),
        in_specs=[vspec(), vspec()],
        out_specs=vspec(),
        compiler_params=params,
        name="final",
    )(x, state)
    return out.reshape(aug, levels, rows_dev, cols_dev)


def solution(mesh):
    placed = (P(None, None, "lat", "lon"), P(), P(), P(), P(), P(), P(None, None, "lat", "lon"))
    return jax.shard_map(
        local, mesh=mesh, in_specs=placed, out_specs=P(None, None, "lat", "lon"), check_vma=False
    )
```

time: 599 us -> 95.2 us (0.16)
  waiting for transfers between devices: 400 us -> 0 us
  matrix products: 104 us -> 0 us
  Pallas kernels: 0 us -> 72 us
  other arithmetic: 43 us -> 6.81 us
  local copies, waits for them, and re-layouts: 31.5 us -> 15.7 us
  between operations: 14.4 us -> 0.15 us
    psum x3 -> x0, waiting for transfers between devices: 369 us -> none  [priors(): return lax.psum(contribution, ('lat', 'lon'))]
    dot_general x69 -> x0, matrix products: 104 us -> none  [the longest x24 56.2 us: assimilate(): prior = jnp.einsum('bij,bj->bi', product, column, precision=HIGH)]
    pallas_call x0 -> x8, Pallas kernels: none -> 72 us  [the longest x3 43.2 us: exchange(): pl.pallas_call(functools.partial(exchange_kernel, digits, cap, offset), o...]
    all_gather x3 -> x0, waiting for transfers between devices: 30.4 us -> none  [local(): transforms = lax.all_gather(partial_maps, 'lon', axis=0, tiled=True)]
    add x24 -> x1, other arithmetic: 16.1 us -> 0.77 us  [local(): pos = slab_of(obs_device, digits, n_lon) * cap + rank]
    select_n x9 -> x2, other arithmetic: 13.4 us -> 0.1 us  [the longest x1 0.09 us: local(): jnp.where(lanes == aug, value_own, jnp.where(lanes == aug + 1, error_own,...]
    gather x18 -> x3, local copies, waits for them, and re-layouts: 20.3 us -> 13.5 us  [local(): pos_sorted = jnp.take_along_axis(pos, obs_order, axis=1)]
    mul x48 -> x0, other arithmetic: 6.77 us -> none  [the longest x24 5.01 us: assimilate(): factor_gain * innovation]
  transfers between devices with their start and end apart: 6 -> 0, of which waited for: 6 -> 0; matrix products, arithmetic and copies ran while one was open for 2% -> 0% of each run, Pallas kernels for 0% -> 0%
where the time goes in v1:
time: 95.2 us; the launch traced here: 94.6 us
  Pallas kernels  72 us (76%)
  local copies, waits for them, and re-layouts  15.7 us (16%)
  other arithmetic  6.81 us (7%)
    pallas_call x3, Pallas kernels, exchange(): pl.pallas_call(functools.partial(exchange_kernel, digits, cap, offset), o...  43.2 us
    pallas_call x3, Pallas kernels, local(): pl.pallas_call(functools.partial(update_kernel, batch, per_block, members...  19.6 us
    gather x3, local copies, waits for them, and re-layouts, local(): pos_sorted = jnp.take_along_axis(pos, obs_order, axis=1)  13.5 us
    pallas_call x1, Pallas kernels, local(): pl.pallas_call(functools.partial(pick_kernel, nbatch, cap, capp, aug, per...  8.61 us

profile of v1, /device:TPU:0, one launch (start us, length us, event | category | flops | bytes accessed | tf_op | source)
XLA Modules:
  0.0 94.6 jit_solution(18121063187346379511)
XLA Ops:
  0.0 0.7 broadcast_compare_fusion
  0.7 0.7 broadcast_compare_fusion.1
  1.4 0.1 convert_reduce_fusion.2
  1.5 0.7 bitcast_or_fusion
  2.2 0.1 convert_reduce_fusion.1
  2.4 0.2 select_reduce_fusion.3.list_ref
  2.5 0.1 iota_compare_fusion
  2.6 1.6 %convert_reduce_fusion = s32[3,512]{1,0:T(4,128)S(1)} fusion(s32[3,512]{1,0:T(4,128)} %param.10, pred[512,512]{1,0:T(8,128)(4,1)S(1)} %iota_compare_fusion), kind=kLoop, calls=%fused_computation.1 | loop fusion | flops 3144192 | bytes 274432 | tf_op jit(solution)/shard_map/reduce_sum | solution.py:256
  4.3 0.9 select_reduce_fusion.2
  5.1 0.1 reshape.82.cells_ref
  5.2 0.8 select_reduce_fusion.1
  6.1 0.8 fusion.8
  6.8 0.0 copy-start.1
  6.8 0.0 copy-start
  6.9 13.4 %gather_fusion = s32[1536]{0:T(1024)S(1)} fusion(s32[3,512]{1,0:T(4,128)S(1)} %fusion.8, s32[1536]{0:T(1024)S(1)} %reshape.88), kind=kCustom, calls=%fused_computation | custom fusion | bytes 24576 | tf_op jit(solution)/shard_map/jit(take_along_axis)/gather | solution.py:258
  20.3 0.0 copy-done.1
  20.3 0.1 broadcast_in_dim.114
  20.4 0.1 broadcast_in_dim.118
  20.5 0.1 select_select_fusion.extra_ref
  20.6 0.0 copy-done
  20.6 0.6 reshape.83.state_ref
  21.2 8.6 %pick.1.x_ref = f32[224,128]{1,0:T(8,128)S(1)} custom-call(s32[96]{0:T(128)S(1)} %reshape.82.cells_ref, f32[1620,128]{1,0:T(8,128)S(1)} %reshape.83.state_ref, f32[96,128]{1,0:T(8,128)S(1)} %select_select_fusion.extra_ref), custom_call_target="tpu_custom_call" | custom-call | tf_op jit(solution)/shard_map/pick/pallas_call | solution.py:278
  29.8 16.3 %exchange.3 = f32[2,2,2,4,32,128]{5,4,3,2,1,0:T(8,128)S(1)} custom-call(f32[224,128]{1,0:T(8,128)S(1)} %pick.1.x_ref), custom_call_target="tpu_custom_call" | custom-call | tf_op jit(solution)/shard_map/exchange/pallas_call | solution.py:141
  46.1 6.4 %update.3.x_ref = f32[224,128]{1,0:T(8,128)S(1)} custom-call(s32[3]{0:T(128)S(1)} %get-tuple-element.7.count_ref, s32[3,64]{1,0:T(4,128)S(1)} %select_reduce_fusion.3.list_ref, s32[3,512]{1,0:T(4,128)S(1)} %and_select_fusion.pos_ref, f32[224,128]{1,0:T(8,128)S(1)} %pick.1.x_ref, f32[1024,128]{1,0:T(8,128)S(1)} %bitcast.11), custom_call_target="tpu_custom_call" | custom-call | tf_op jit(solution)/shard_map/update/pallas_call | solution.py:289
  52.5 13.4 %exchange.4 = f32[2,2,2,4,32,128]{5,4,3,2,1,0:T(8,128)S(1)} custom-call(f32[224,128]{1,0:T(8,128)S(1)} %update.3.x_ref), custom_call_target="tpu_custom_call" | custom-call | tf_op jit(solution)/shard_map/exchange/pallas_call | solution.py:141
  65.9 6.6 %update.4.x_ref = f32[224,128]{1,0:T(8,128)S(1)} custom-call(s32[3]{0:T(128)S(1)} %get-tuple-element.7.count_ref, s32[3,64]{1,0:T(4,128)S(1)} %select_reduce_fusion.3.list_ref, s32[3,512]{1,0:T(4,128)S(1)} %and_select_fusion.pos_ref, f32[224,128]{1,0:T(8,128)S(1)} %update.3.x_ref, f32[1024,128]{1,0:T(8,128)S(1)} %bitcast.12), custom_call_target="tpu_custom_call" | custom-call | tf_op jit(solution)/shard_map/update/pallas_call | solution.py:289
  72.5 13.5 %exchange.5 = f32[2,2,2,4,32,128]{5,4,3,2,1,0:T(8,128)S(1)} custom-call(f32[224,128]{1,0:T(8,128)S(1)} %update.4.x_ref), custom_call_target="tpu_custom_call" | custom-call | tf_op jit(solution)/shard_map/exchange/pallas_call | solution.py:141
  86.0 6.6 %update.5.x_ref = f32[224,128]{1,0:T(8,128)S(1)} custom-call(s32[3]{0:T(128)S(1)} %get-tuple-element.7.count_ref, s32[3,64]{1,0:T(4,128)S(1)} %select_reduce_fusion.3.list_ref, s32[3,512]{1,0:T(4,128)S(1)} %and_select_fusion.pos_ref, f32[224,128]{1,0:T(8,128)S(1)} %update.4.x_ref, f32[1024,128]{1,0:T(8,128)S(1)} %bitcast.10), custom_call_target="tpu_custom_call" | custom-call | tf_op jit(solution)/shard_map/update/pallas_call | solution.py:289
  92.6 0.6 final.1
  93.2 1.4 %reshape.87 = f32[81,10,2,128]{3,2,1,0:T(2,128)} reshape(f32[1620,128]{1,0:T(8,128)S(1)} %final.1) | data formatting | bytes 1658880 | tf_op jit(solution)/shard_map/reshape | solution.py:307
  (5 shorter events, 0.0 us)
Async XLA Ops:
  6.8 13.5 %copy-start.1 = (s32[3,512]{1,0:T(4,128)S(1)}, s32[3,512]{1,0:T(4,128)}, u32[]{:S(2)}) copy-start(s32[3,512]{1,0:T(4,128)} %param.12) | copy-start | bytes 18436
  6.8 13.8 %copy-start = (f32[81,10,2,128]{3,2,1,0:T(2,128)S(1)}, f32[81,10,2,128]{3,2,1,0:T(2,128)}, u32[]{:S(2)}) copy-start(f32[81,10,2,128]{3,2,1,0:T(2,128)} %param.7) | copy-start | bytes 2488324

commit v2 on v1

v2 whole, which is shorter than its diff:
```python
import functools
import jax
import jax.numpy as jnp
from jax import lax
from jax.experimental import pallas as pl
from jax.experimental.pallas import tpu as pltpu
from jax.sharding import PartitionSpec as P

MESH = pl.DeviceIdType.MESH
GROUP = 32
LANES = 128
VMEM_LIMIT = 32 * 1024 * 1024


def digits_of(n_lat, n_lon):
    def factors(size):
        out, stride = [], 1
        while size > 1:
            f = 4 if size % 4 == 0 else (2 if size % 2 == 0 else size)
            out.append((stride, f))
            stride, size = stride * f, size // f
        return out
    if (n_lat, n_lon) == (16, 2):
        return [("lat", 4, 4), ("lat", 1, 2), ("lat", 2, 2), ("lon", 1, 2)]
    return [("lon", s, f) for s, f in factors(n_lon)] + [("lat", s, f) for s, f in factors(n_lat)]


def split2(a):
    hi = a.astype(jnp.bfloat16)
    return hi, (a - hi.astype(jnp.float32)).astype(jnp.bfloat16)


def mm3(a, b, dims=((1,), (0,))):
    ah, al = a if isinstance(a, tuple) else split2(a)
    bh, bl = b if isinstance(b, tuple) else split2(b)
    dot = functools.partial(
        lax.dot_general, dimension_numbers=(dims, ((), ())), preferred_element_type=jnp.float32
    )
    return dot(ah, bh) + (dot(ah, bl) + dot(al, bh))


NT = ((1,), (1,))


def pow2_part(value, stride, size):
    return (value >> (stride.bit_length() - 1)) & (size - 1)


def exchange_body(digits, fill, meanwhile, buf_ref, send_sem, recv_sem):
    place = {axis: lax.axis_index(axis) for axis in ("lat", "lon")}
    mine = [lax.rem(place[axis] // stride, size) for axis, stride, size in digits]

    def peer(*moves):
        moved = dict(place)
        for which, step in moves:
            axis, stride, size = digits[which]
            other = lax.rem(mine[which] + step, size)
            moved[axis] = moved[axis] + (other - mine[which]) * stride
        return (moved["lat"], moved["lon"])

    grid = [size for _, _, size in digits] == [4, 2, 2, 2]
    partners = [((which, step),) for which, (_, _, size) in enumerate(digits) for step in range(1, size)]
    if grid:
        partners.append(((1, 1), (2, 1)))
    barrier = pltpu.get_barrier_semaphore()
    for moves in partners:
        pl.semaphore_signal(barrier, inc=1, device_id=peer(*moves), device_id_type=MESH)
    own = tuple(mine[::-1])
    buf_ref[own] = fill()
    pl.semaphore_wait(barrier, len(partners))

    sends = []

    def send(part, device):
        slot = len(sends)
        copy = pltpu.make_async_remote_copy(
            src_ref=buf_ref.at[part], dst_ref=buf_ref.at[part],
            send_sem=send_sem.at[slot], recv_sem=recv_sem.at[slot],
            device_id=device, device_id_type=MESH,
        )
        copy.start()
        sends.append(copy)
        return copy

    if grid:
        z, x, y, k = mine
        plane = [peer((1, 1)), peer((2, 1)), peer((1, 1), (2, 1))]
        other = peer((3, 1))
        line = [(step, send((k, y, x, z), peer((0, step)))) for step in (1, 3, 2)]
        arriving = [[send((k, y, x, z), device)] for device in plane]
        meanwhile()
        for step, copy in line:
            copy.wait_recv()
            chunk = lax.rem(z + 4 - step, 4)
            for place_now, device in enumerate(plane):
                arriving[place_now].append(send((k, y, x, chunk), device))
        last = [send((k, y, x), other)]
        for copies, (yy, xx) in zip(arriving, ((y, 1 - x), (1 - y, x), (1 - y, 1 - x))):
            for copy in copies:
                copy.wait_recv()
            last.append(send((k, yy, xx), other))
        for copy in last:
            copy.wait_recv()
    else:
        for which, (_, _, size) in enumerate(digits):
            part = tuple(mine[which:][::-1])
            stage = [send(part, peer((which, step))) for step in range(1, size)]
            if which == 0:
                meanwhile()
            for copy in stage:
                copy.wait_recv()
    for copy in sends:
        copy.wait_send()


def exchange_kernel(digits, cap, offset, x_ref, buf_ref, send_sem, recv_sem):
    exchange_body(
        digits, lambda: x_ref[offset:offset + cap, :], lambda: None, buf_ref, send_sem, recv_sem
    )


def exchange_scratch(digits):
    copies = 19 if [s for _, _, s in digits] == [4, 2, 2, 2] else sum(s - 1 for _, _, s in digits)
    return [pltpu.SemaphoreType.DMA((copies,)), pltpu.SemaphoreType.DMA((copies,))]


def buffer_shape(digits, cap):
    return jax.ShapeDtypeStruct(
        tuple(size for _, _, size in digits[::-1]) + (cap, LANES), jnp.float32
    )


def exchange(x, digits, cap, offset, ident):
    return pl.pallas_call(
        functools.partial(exchange_kernel, digits, cap, offset),
        out_shape=buffer_shape(digits, cap),
        in_specs=[vspec()],
        out_specs=vspec(),
        scratch_shapes=exchange_scratch(digits),
        compiler_params=pltpu.CompilerParams(
            collective_id=ident, has_side_effects=True, vmem_limit_bytes=VMEM_LIMIT
        ),
        name="exchange",
    )(x)


def first_kernel(digits, cap, capp, aug, per_member, base, values_ref, errors_ref, device_ref, cell_ref,
                 state_ref, buf_ref, x_ref, pos_ref, send_sem, recv_sem):
    nbatch, nobs = device_ref.shape
    n_lat, n_lon = lax.axis_size("lat"), lax.axis_size("lon")
    ndev = n_lat * n_lon
    me = lax.axis_index("lat") * n_lon + lax.axis_index("lon")
    earlier = (
        lax.broadcasted_iota(jnp.int32, (nobs, nobs), 0) < lax.broadcasted_iota(jnp.int32, (nobs, nobs), 1)
    ).astype(jnp.float32).astype(jnp.bfloat16)

    def ranks(flags):
        return jnp.dot(flags.astype(jnp.bfloat16), earlier, preferred_element_type=jnp.float32)

    def fill():
        owned = (device_ref[...] == me).astype(jnp.float32)
        rank = ranks(owned)
        slot = lax.broadcasted_iota(jnp.int32, (capp, nobs), 0).astype(jnp.float32)
        lane = lax.broadcasted_iota(jnp.int32, (capp, LANES), 1)
        cells = []
        for batch in range(nbatch):
            row = slice(batch, batch + 1)
            chosen = (rank[row] == slot) & (owned[row] > 0)

            def total(ref):
                return jnp.sum(jnp.where(chosen, ref[row, :].astype(jnp.float32), 0.0), axis=1, keepdims=True)

            cells.append(total(cell_ref))
            x_ref[base + batch * capp:base + (batch + 1) * capp, :] = jnp.where(
                lane == aug, total(values_ref), jnp.where(lane == aug + 1, total(errors_ref), 0.0)
            )
        cell = jnp.concatenate(cells, axis=0).astype(jnp.int32)
        wide = 2 * LANES
        spot = lax.broadcasted_iota(jnp.int32, (nbatch * capp, wide), 1)
        picked = jnp.zeros((nbatch * capp, aug), jnp.float32)
        for j in range(0, per_member, 2):
            cut = jnp.concatenate(
                [state_ref[pl.ds(j + k, aug, stride=per_member), :] for k in range(2)], axis=1
            )
            mark = (spot + j * LANES == cell).astype(jnp.float32).astype(jnp.bfloat16)
            for _ in range(3):
                part = cut.astype(jnp.bfloat16)
                picked = picked + lax.dot_general(
                    mark, part, (NT, ((), ())), preferred_element_type=jnp.float32
                )
                cut = cut - part.astype(jnp.float32)
        x_ref[base:base + nbatch * capp, 0:aug] = picked
        return x_ref[base:base + cap, :]

    def meanwhile():
        x_ref[0:base, :] = (
            lax.broadcasted_iota(jnp.int32, (base, LANES), 0)
            == lax.broadcasted_iota(jnp.int32, (base, LANES), 1)
        ).astype(jnp.float32)
        names = lax.broadcasted_iota(jnp.int32, (ndev, nobs), 0)
        for batch in range(nbatch):
            device = device_ref[batch:batch + 1, :]
            held = (device == names).astype(jnp.float32)
            rank = jnp.sum(held * ranks(held), axis=0, keepdims=True)
            place = {"lat": device >> (n_lon.bit_length() - 1), "lon": device & (n_lon - 1)}
            slab, weight = jnp.zeros_like(device), 1
            for axis, stride, size in digits:
                slab = slab + pow2_part(place[axis], stride, size) * weight
                weight *= size
            pos_ref[batch:batch + 1, :] = slab * cap + rank.astype(jnp.int32)

    exchange_body(digits, fill, meanwhile, buf_ref, send_sem, recv_sem)


def group_update(z, valid, x, per_block, members):
    lane = lax.broadcasted_iota(jnp.int32, (GROUP, LANES), 1)
    is_member = (lane >= 1) & (lane <= members)
    z = list(z)
    hs, vs, ws = [], [], []
    for i in range(per_block):
        p = z[i]
        h = jnp.where(is_member, p, 0.0)
        s = jnp.sum(h * h, axis=1, keepdims=True) / (members - 1)
        y = p[:, members + 1:members + 2]
        r = p[:, members + 2:members + 3]
        q = s + r
        c = 1.0 / ((members - 1) * q)
        a = 1.0 / (1.0 + jnp.sqrt(r / q))
        d = y - p[:, 0:1]
        v = jnp.where(lane == 0, c * d, -(a * c) * h)
        for j in range(i + 1, per_block):
            z[j] = z[j] + v * jnp.sum(h * z[j], axis=1, keepdims=True)
        w = h
        for j in range(i):
            w = w + ws[j] * jnp.sum(h * vs[j], axis=1, keepdims=True)
        vs.append(v)
        ws.append(w)
    v_all = split2(jnp.concatenate([v * valid for v in vs], axis=0))
    w_all = split2(jnp.concatenate(ws, axis=0))
    size = per_block * GROUP
    upper = mm3(v_all, w_all, NT)
    row = lax.broadcasted_iota(jnp.int32, (size, size), 0) & (GROUP - 1)
    col = lax.broadcasted_iota(jnp.int32, (size, size), 1) & (GROUP - 1)
    differ = row ^ col
    levels = GROUP.bit_length() - 1
    ahead = row < col
    inverse = jnp.where(
        lax.broadcasted_iota(jnp.int32, (size, size), 0)
        == lax.broadcasted_iota(jnp.int32, (size, size), 1), 1.0,
        jnp.where(ahead & (differ == 1), upper, 0.0),
    )
    for level in range(1, levels):
        pairs = ahead & (differ >= (1 << level)) & (differ < (2 << level))
        parts = split2(inverse)
        inverse = inverse + mm3(mm3(parts, jnp.where(pairs, upper, 0.0)), parts)
    return x + mm3(mm3(mm3(x, w_all, NT), inverse), v_all)


def update_kernel(batch, per_block, members, coupled_ref, order_ref, pos_ref, x_ref, buf_ref, out_ref, z_ref, list_ref):
    out_ref[...] = x_ref[...]
    total = jnp.int32(0)
    for block in range(coupled_ref.shape[1]):
        list_ref[total] = block
        total = total + (coupled_ref[batch, block] > 0).astype(jnp.int32)

    @pl.loop(0, (total + GROUP - 1) // GROUP)
    def _(group):
        start = group * GROUP

        @pl.loop(0, GROUP, unroll=8)
        def _(b):
            block = list_ref[jnp.minimum(start + b, total - 1)]
            for i in range(per_block):
                source = pos_ref[batch, order_ref[batch, block * per_block + i]]
                z_ref[pl.ds(i * GROUP + b, 1), :] = buf_ref[pl.ds(source, 1), :]

        valid = (
            start + lax.broadcasted_iota(jnp.int32, (GROUP, 1), 0) < total
        ).astype(jnp.float32)
        z = [z_ref[i * GROUP:(i + 1) * GROUP, :] for i in range(per_block)]
        out_ref[...] = group_update(z, valid, out_ref[...], per_block, members)


def final_kernel(aug, per_member, x_ref, state_ref, out_ref):
    turned = jnp.transpose(x_ref[0:LANES, :])
    parts = split2(turned[0:aug, 0:aug])
    for j in range(0, per_member, 2):
        cut = [state_ref[pl.ds(j + k, aug, stride=per_member), :] for k in range(2)]
        new = mm3(parts, jnp.concatenate(cut, axis=1))
        for k in range(2):
            out_ref[pl.ds(j + k, aug, stride=per_member), :] = new[:, k * LANES:(k + 1) * LANES]


def vspec():
    return pl.BlockSpec(memory_space=pltpu.VMEM)


def sspec():
    return pl.BlockSpec(memory_space=pltpu.SMEM)


def local(ensemble, obs_values, obs_errors, obs_device, obs_cell, obs_order, coupling):
    aug, levels, rows_dev, cols_dev = ensemble.shape
    members = aug - 1
    n_lat, n_lon = lax.axis_size("lat"), lax.axis_size("lon")
    ndev = n_lat * n_lon
    nbatch, nobs = obs_values.shape
    nblocks = coupling.shape[1]
    per_block = nobs // nblocks
    cap = max(1, 2 * nobs // ndev)
    capp = -(-cap // 8) * 8
    digits = digits_of(n_lat, n_lon)
    per_member = levels * rows_dev * cols_dev // LANES
    state = ensemble.reshape(aug * per_member, LANES)
    params = pltpu.CompilerParams(vmem_limit_bytes=VMEM_LIMIT)

    coupled = coupling.reshape(nbatch, nblocks)
    base = LANES
    rows = base + nbatch * capp
    buf, x, pos = pl.pallas_call(
        functools.partial(first_kernel, digits, cap, capp, aug, per_member, base),
        out_shape=(
            buffer_shape(digits, cap),
            jax.ShapeDtypeStruct((rows, LANES), jnp.float32),
            jax.ShapeDtypeStruct((nbatch, nobs), jnp.int32),
        ),
        in_specs=[vspec()] * 5,
        out_specs=(vspec(),) * 3,
        scratch_shapes=exchange_scratch(digits),
        compiler_params=pltpu.CompilerParams(
            collective_id=0, has_side_effects=True, vmem_limit_bytes=VMEM_LIMIT
        ),
        name="first",
    )(obs_values, obs_errors, obs_device, obs_cell, state)

    for batch in range(nbatch):
        if batch > 0:
            buf = exchange(x, digits, cap, base + batch * capp, batch)
        x = pl.pallas_call(
            functools.partial(update_kernel, batch, per_block, members),
            out_shape=jax.ShapeDtypeStruct((rows, LANES), jnp.float32),
            in_specs=[sspec(), sspec(), sspec(), vspec(), vspec()],
            out_specs=vspec(),
            scratch_shapes=[
                pltpu.VMEM((per_block * GROUP, LANES), jnp.float32),
                pltpu.SMEM((nblocks + 1,), jnp.int32),
            ],
            compiler_params=params,
            name="update",
        )(coupled, obs_order, pos, x, buf.reshape(ndev * cap, LANES))

    out = pl.pallas_call(
        functools.partial(final_kernel, aug, per_member),
        out_shape=jax.ShapeDtypeStruct((aug * per_member, LANES), jnp.float32),
        in_specs=[vspec(), vspec()],
        out_specs=vspec(),
        compiler_params=params,
        name="final",
    )(x, state)
    return out.reshape(aug, levels, rows_dev, cols_dev)


def solution(mesh):
    placed = (P(None, None, "lat", "lon"), P(), P(), P(), P(), P(), P(None, None, "lat", "lon"))
    return jax.shard_map(
        local, mesh=mesh, in_specs=placed, out_specs=P(None, None, "lat", "lon"), check_vma=False
    )
```

time: 95.2 us -> 61.6 us (0.65)
  Pallas kernels: 72 us -> 57.5 us
  local copies, waits for them, and re-layouts: 15.7 us -> 3.85 us
  other arithmetic: 6.81 us -> 0 us
    pallas_call x3 -> x2, Pallas kernels: 43.2 us -> 21.8 us  [exchange(): pl.pallas_call(functools.partial(exchange_kernel, digits, cap, offset), o...]
    gather x3 -> x0, local copies, waits for them, and re-layouts: 13.5 us -> none  [local(): pos_sorted = jnp.take_along_axis(pos, obs_order, axis=1)]
    pallas_call x1, Pallas kernels: 8.61 us -> 14.2 us  [local(): pl.pallas_call(functools.partial(first_kernel, digits, cap, capp, aug, pe...]
    reduce_sum x6 -> x0, other arithmetic: 3.75 us -> none  [the longest x1 1.63 us: local(): rank = jnp.sum((same & before[None]).astype(jnp.int32), axis=2)]
    pallas_call x3, Pallas kernels: 19.6 us -> 20.9 us  [local(): pl.pallas_call(functools.partial(update_kernel, batch, per_block, members...]
    reshape x1, local copies, waits for them, and re-layouts: 0.57 us -> 1.77 us  [local(): state = ensemble.reshape(aug * per_member, LANES)]
where the time goes in v2:
time: 61.6 us; the launch traced here: 61.4 us
  Pallas kernels  57.5 us (93%)
  local copies, waits for them, and re-layouts  3.85 us (6%)
    pallas_call x2, Pallas kernels, exchange(): pl.pallas_call(functools.partial(exchange_kernel, digits, cap, offset), o...  21.8 us
    pallas_call x3, Pallas kernels, local(): pl.pallas_call(functools.partial(update_kernel, batch, per_block, members...  20.9 us
    pallas_call x1, Pallas kernels, local(): pl.pallas_call(functools.partial(first_kernel, digits, cap, capp, aug, pe...  14.2 us
    reshape x1, local copies, waits for them, and re-layouts, local(): state = ensemble.reshape(aug * per_member, LANES)  1.77 us
    reshape x1, local copies, waits for them, and re-layouts, local(): return out.reshape(aug, levels, rows_dev, cols_dev)  1.38 us

profile of v2, /device:TPU:0, one launch (start us, length us, event | category | flops | bytes accessed | tf_op | source)
XLA Modules:
  0.0 61.4 jit_solution(3134305761033224701)
XLA Ops:
  0.0 0.7 %copy.10 = s32[3,64,1,1]{1,0,2,3:T(4,128)S(1)} copy(s32[3,64,1,1]{1,3,2,0:T(1,128)} %param.13) | data formatting | bytes 1536
  0.7 0.0 copy-start.1
  0.7 0.0 copy-start.2
  0.7 0.0 copy-start.3
  0.7 0.0 copy-start.4
  0.7 1.8 %reshape.19.state_ref = f32[1620,128]{1,0:T(8,128)S(1)} reshape(f32[81,10,2,128]{3,2,1,0:T(2,128)} %param.7) | data formatting | bytes 1658880 | tf_op jit(solution)/shard_map/reshape | solution.py:314
  2.5 0.0 copy-done.1
  2.5 0.0 copy-done.2
  2.5 0.0 copy-done.3
  2.5 0.0 copy-done.4
  2.5 0.0 copy-start
  2.5 14.2 %first.1 = (f32[2,2,2,4,32,128]{5,4,3,2,1,0:T(8,128)S(1)}, f32[224,128]{1,0:T(8,128)S(1)}, s32[3,512]{1,0:T(4,128)S(1)}) custom-call(f32[3,512]{1,0:T(4,128)S(1)} %copy-done.1, f32[3,512]{1,0:T(4,128)S(1)} %copy-done.2, s32[3,512]{1,0:T(4,128)S(1)} %copy-done.3, s32[3,512]{1,0:T(4,128)S(1)} %copy-done.4, f32[1620,128]{1,0:T(8,128)S(1)} %reshape.19.state_ref), custom_call_target="tpu_custom_call" | custom-call | tf_op jit(solution)/shard_map/first/pallas_call | solution.py:320
  16.7 0.0 copy-done
  16.8 6.9 %update.3.x_ref = f32[224,128]{1,0:T(8,128)S(1)} custom-call(s32[3,64]{1,0:T(4,128)S(1)} %bitcast.9, s32[3,512]{1,0:T(4,128)S(1)} %copy-done, s32[3,512]{1,0:T(4,128)S(1)} %get-tuple-element.8.pos_ref, f32[224,128]{1,0:T(8,128)S(1)} %get-tuple-element.9.x_ref, f32[1024,128]{1,0:T(8,128)S(1)} %bitcast.8), custom_call_target="tpu_custom_call" | custom-call | tf_op jit(solution)/shard_map/update/pallas_call | solution.py:339
  23.6 11.3 %exchange.2 = f32[2,2,2,4,32,128]{5,4,3,2,1,0:T(8,128)S(1)} custom-call(f32[224,128]{1,0:T(8,128)S(1)} %update.3.x_ref), custom_call_target="tpu_custom_call" | custom-call | tf_op jit(solution)/shard_map/exchange/pallas_call | solution.py:134
  34.9 7.0 %update.4.x_ref = f32[224,128]{1,0:T(8,128)S(1)} custom-call(s32[3,64]{1,0:T(4,128)S(1)} %bitcast.10, s32[3,512]{1,0:T(4,128)S(1)} %copy-done, s32[3,512]{1,0:T(4,128)S(1)} %get-tuple-element.8.pos_ref, f32[224,128]{1,0:T(8,128)S(1)} %update.3.x_ref, f32[1024,128]{1,0:T(8,128)S(1)} %bitcast.7), custom_call_target="tpu_custom_call" | custom-call | tf_op jit(solution)/shard_map/update/pallas_call | solution.py:339
  41.9 10.5 %exchange.3 = f32[2,2,2,4,32,128]{5,4,3,2,1,0:T(8,128)S(1)} custom-call(f32[224,128]{1,0:T(8,128)S(1)} %update.4.x_ref), custom_call_target="tpu_custom_call" | custom-call | tf_op jit(solution)/shard_map/exchange/pallas_call | solution.py:134
  52.4 7.0 %update.5.x_ref = f32[224,128]{1,0:T(8,128)S(1)} custom-call(s32[3,64]{1,0:T(4,128)S(1)} %bitcast.11, s32[3,512]{1,0:T(4,128)S(1)} %copy-done, s32[3,512]{1,0:T(4,128)S(1)} %get-tuple-element.8.pos_ref, f32[224,128]{1,0:T(8,128)S(1)} %update.4.x_ref, f32[1024,128]{1,0:T(8,128)S(1)} %bitcast.6), custom_call_target="tpu_custom_call" | custom-call | tf_op jit(solution)/shard_map/update/pallas_call | solution.py:339
  59.4 0.6 final.1
  60.0 1.4 %reshape.23 = f32[81,10,2,128]{3,2,1,0:T(2,128)} reshape(f32[1620,128]{1,0:T(8,128)S(1)} %final.1) | data formatting | bytes 1658880 | tf_op jit(solution)/shard_map/reshape | solution.py:360
Async XLA Ops:
  0.7 1.8 %copy-start.1 = (f32[3,512]{1,0:T(4,128)S(1)}, f32[3,512]{1,0:T(4,128)}, u32[]{:S(2)}) copy-start(f32[3,512]{1,0:T(4,128)} %values_ref.1) | copy-start | bytes 18436
  0.7 1.8 %copy-start.2 = (f32[3,512]{1,0:T(4,128)S(1)}, f32[3,512]{1,0:T(4,128)}, u32[]{:S(2)}) copy-start(f32[3,512]{1,0:T(4,128)} %errors_ref.1) | copy-start | bytes 18436
  0.7 1.8 %copy-start.3 = (s32[3,512]{1,0:T(4,128)S(1)}, s32[3,512]{1,0:T(4,128)}, u32[]{:S(2)}) copy-start(s32[3,512]{1,0:T(4,128)} %device_ref.1) | copy-start | bytes 18436
  0.7 1.8 %copy-start.4 = (s32[3,512]{1,0:T(4,128)S(1)}, s32[3,512]{1,0:T(4,128)}, u32[]{:S(2)}) copy-start(s32[3,512]{1,0:T(4,128)} %cell_ref.1) | copy-start | bytes 18436
  2.5 14.2 %copy-start = (s32[3,512]{1,0:T(4,128)S(1)}, s32[3,512]{1,0:T(4,128)}, u32[]{:S(2)}) copy-start(s32[3,512]{1,0:T(4,128)} %order_ref.5) | copy-start | bytes 18436

commit v3 on v2

--- a/solution.py
+++ b/solution.py
@@ -1,4 +1,5 @@
 import functools
+import itertools
 import jax
 import jax.numpy as jnp
 from jax import lax
@@ -46,7 +47,11 @@
     return (value >> (stride.bit_length() - 1)) & (size - 1)
 
 
-def exchange_body(digits, fill, meanwhile, buf_ref, send_sem, recv_sem):
+def fold_of(cap, width):
+    return 24 if cap == 32 and LANES - width >= (width + 1) // 2 else cap
+
+
+def exchange_body(digits, cap, width, fill, meanwhile, buf_ref, send_sem, recv_sem):
     place = {axis: lax.axis_index(axis) for axis in ("lat", "lon")}
     mine = [lax.rem(place[axis] // stride, size) for axis, stride, size in digits]
 
@@ -66,13 +71,26 @@
     for moves in partners:
         pl.semaphore_signal(barrier, inc=1, device_id=peer(*moves), device_id_type=MESH)
     own = tuple(mine[::-1])
-    buf_ref[own] = fill()
+    sent = fold_of(cap, width)
+    half = (width + 1) // 2
+    chunk_now = fill()
+    if sent < cap:
+        tail = chunk_now[24:32]
+        lane = lax.broadcasted_iota(jnp.int32, tail.shape, 1)
+        low = jnp.where(lane < half, tail, 0.0)
+        high = jnp.where((lane >= half) & (lane < width), tail, 0.0)
+        buf_ref[own + (slice(0, 8),)] = chunk_now[0:8] + pltpu.roll(low, width, 1)
+        buf_ref[own + (slice(8, 16),)] = chunk_now[8:16] + pltpu.roll(high, width - half, 1)
+        buf_ref[own + (slice(16, 24),)] = chunk_now[16:24]
+    else:
+        buf_ref[own] = chunk_now
     pl.semaphore_wait(barrier, len(partners))
 
     sends = []
 
     def send(part, device):
         slot = len(sends)
+        part = part + (slice(None),) * (len(digits) - len(part)) + (pl.ds(0, sent),)
         copy = pltpu.make_async_remote_copy(
             src_ref=buf_ref.at[part], dst_ref=buf_ref.at[part],
             send_sem=send_sem.at[slot], recv_sem=recv_sem.at[slot],
@@ -111,11 +129,17 @@
                 copy.wait_recv()
     for copy in sends:
         copy.wait_send()
-
-
-def exchange_kernel(digits, cap, offset, x_ref, buf_ref, send_sem, recv_sem):
+    if sent < cap:
+        for spot in itertools.product(*(range(size) for _, _, size in digits[::-1])):
+            low = pltpu.roll(buf_ref[spot + (slice(0, 8),)], LANES - width, 1)
+            high = pltpu.roll(buf_ref[spot + (slice(8, 16),)], LANES - width + half, 1)
+            lane = lax.broadcasted_iota(jnp.int32, low.shape, 1)
+            buf_ref[spot + (slice(24, 32),)] = jnp.where(lane < half, low, high)
+
+
+def exchange_kernel(digits, cap, width, x_ref, buf_ref, send_sem, recv_sem):
     exchange_body(
-        digits, lambda: x_ref[offset:offset + cap, :], lambda: None, buf_ref, send_sem, recv_sem
+        digits, cap, width, lambda: x_ref[0:cap, :], lambda: None, buf_ref, send_sem, recv_sem
     )
 
 
@@ -130,9 +154,9 @@
     )
 
 
-def exchange(x, digits, cap, offset, ident):
+def exchange(x, digits, cap, width, ident):
     return pl.pallas_call(
-        functools.partial(exchange_kernel, digits, cap, offset),
+        functools.partial(exchange_kernel, digits, cap, width),
         out_shape=buffer_shape(digits, cap),
         in_specs=[vspec()],
         out_specs=vspec(),
@@ -171,7 +195,7 @@
                 return jnp.sum(jnp.where(chosen, ref[row, :].astype(jnp.float32), 0.0), axis=1, keepdims=True)
 
             cells.append(total(cell_ref))
-            x_ref[base + batch * capp:base + (batch + 1) * capp, :] = jnp.where(
+            x_ref[batch * capp:(batch + 1) * capp, :] = jnp.where(
                 lane == aug, total(values_ref), jnp.where(lane == aug + 1, total(errors_ref), 0.0)
             )
         cell = jnp.concatenate(cells, axis=0).astype(jnp.int32)
@@ -189,13 +213,13 @@
                     mark, part, (NT, ((), ())), preferred_element_type=jnp.float32
                 )
                 cut = cut - part.astype(jnp.float32)
-        x_ref[base:base + nbatch * capp, 0:aug] = picked
-        return x_ref[base:base + cap, :]
+        x_ref[0:base, 0:aug] = picked
+        return x_ref[0:cap, :]
 
     def meanwhile():
-        x_ref[0:base, :] = (
-            lax.broadcasted_iota(jnp.int32, (base, LANES), 0)
-            == lax.broadcasted_iota(jnp.int32, (base, LANES), 1)
+        square = (x_ref.shape[0] - base, LANES)
+        x_ref[base:, :] = (
+            lax.broadcasted_iota(jnp.int32, square, 0) == lax.broadcasted_iota(jnp.int32, square, 1)
         ).astype(jnp.float32)
         names = lax.broadcasted_iota(jnp.int32, (ndev, nobs), 0)
         for batch in range(nbatch):
@@ -209,7 +233,7 @@
                 weight *= size
             pos_ref[batch:batch + 1, :] = slab * cap + rank.astype(jnp.int32)
 
-    exchange_body(digits, fill, meanwhile, buf_ref, send_sem, recv_sem)
+    exchange_body(digits, cap, aug + 2, fill, meanwhile, buf_ref, send_sem, recv_sem)
 
 
 def group_update(z, valid, x, per_block, members):
@@ -235,29 +259,36 @@
             w = w + ws[j] * jnp.sum(h * vs[j], axis=1, keepdims=True)
         vs.append(v)
         ws.append(w)
-    v_all = split2(jnp.concatenate([v * valid for v in vs], axis=0))
-    w_all = split2(jnp.concatenate(ws, axis=0))
-    size = per_block * GROUP
-    upper = mm3(v_all, w_all, NT)
-    row = lax.broadcasted_iota(jnp.int32, (size, size), 0) & (GROUP - 1)
-    col = lax.broadcasted_iota(jnp.int32, (size, size), 1) & (GROUP - 1)
-    differ = row ^ col
-    levels = GROUP.bit_length() - 1
-    ahead = row < col
-    inverse = jnp.where(
-        lax.broadcasted_iota(jnp.int32, (size, size), 0)
-        == lax.broadcasted_iota(jnp.int32, (size, size), 1), 1.0,
-        jnp.where(ahead & (differ == 1), upper, 0.0),
-    )
+    half = GROUP // 2
+    size = per_block * half
+    row_id = lax.broadcasted_iota(jnp.int32, (size, size), 0)
+    col_id = lax.broadcasted_iota(jnp.int32, (size, size), 1)
+    differ = (row_id ^ col_id) & (half - 1)
+    ahead = (row_id & (half - 1)) < (col_id & (half - 1))
+    levels = half.bit_length() - 1
+    vs = [v * valid for v in vs]
+    cuts = [slice(0, half), slice(half, GROUP)]
+    v_half = [split2(jnp.concatenate([v[cut] for v in vs], axis=0)) for cut in cuts]
+    w_half = [split2(jnp.concatenate([w[cut] for w in ws], axis=0)) for cut in cuts]
+    upper = [mm3(v, w, NT) for v, w in zip(v_half, w_half)]
+    across = split2(mm3(v_half[0], w_half[1], NT))
+    x_parts = split2(x)
+    seen = [mm3(x_parts, w, NT) for w in w_half]
+    inverse = [
+        jnp.where(row_id == col_id, 1.0, jnp.where(ahead & (differ == 1), u, 0.0)) for u in upper
+    ]
     for level in range(1, levels):
         pairs = ahead & (differ >= (1 << level)) & (differ < (2 << level))
-        parts = split2(inverse)
-        inverse = inverse + mm3(mm3(parts, jnp.where(pairs, upper, 0.0)), parts)
-    return x + mm3(mm3(mm3(x, w_all, NT), inverse), v_all)
-
-
-def update_kernel(batch, per_block, members, coupled_ref, order_ref, pos_ref, x_ref, buf_ref, out_ref, z_ref, list_ref):
-    out_ref[...] = x_ref[...]
+        parts = [split2(i) for i in inverse]
+        inner = [mm3(p, jnp.where(pairs, u, 0.0)) for p, u in zip(parts, upper)]
+        inverse = [i + mm3(m, p) for i, m, p in zip(inverse, inner, parts)]
+    first = split2(mm3(seen[0], inverse[0]))
+    second = mm3(seen[1] + mm3(first, across), inverse[1])
+    return x + (mm3(first, v_half[0]) + mm3(second, v_half[1]))
+
+
+def update_kernel(batch, per_block, members, capp, coupled_ref, order_ref, pos_ref, x_ref, buf_ref, out_ref, z_ref, list_ref):
+    out_ref[...] = x_ref[capp:, :]
     total = jnp.int32(0)
     for block in range(coupled_ref.shape[1]):
         list_ref[total] = block
@@ -282,7 +313,8 @@
 
 
 def final_kernel(aug, per_member, x_ref, state_ref, out_ref):
-    turned = jnp.transpose(x_ref[0:LANES, :])
+    rest = jnp.zeros((LANES - x_ref.shape[0], LANES), jnp.float32)
+    turned = jnp.transpose(jnp.concatenate([x_ref[...], rest], axis=0))
     parts = split2(turned[0:aug, 0:aug])
     for j in range(0, per_member, 2):
         cut = [state_ref[pl.ds(j + k, aug, stride=per_member), :] for k in range(2)]
@@ -315,8 +347,8 @@
     params = pltpu.CompilerParams(vmem_limit_bytes=VMEM_LIMIT)
 
     coupled = coupling.reshape(nbatch, nblocks)
-    base = LANES
-    rows = base + nbatch * capp
+    base = nbatch * capp
+    rows = base + -(-aug // 16) * 16
     buf, x, pos = pl.pallas_call(
         functools.partial(first_kernel, digits, cap, capp, aug, per_member, base),
         out_shape=(
@@ -335,10 +367,10 @@
 
     for batch in range(nbatch):
         if batch > 0:
-            buf = exchange(x, digits, cap, base + batch * capp, batch)
+            buf = exchange(x, digits, cap, aug + 2, batch)
         x = pl.pallas_call(
-            functools.partial(update_kernel, batch, per_block, members),
-            out_shape=jax.ShapeDtypeStruct((rows, LANES), jnp.float32),
+            functools.partial(update_kernel, batch, per_block, members, capp),
+            out_shape=jax.ShapeDtypeStruct((rows - (batch + 1) * capp, LANES), jnp.float32),
             in_specs=[sspec(), sspec(), sspec(), vspec(), vspec()],
             out_specs=vspec(),
             scratch_shapes=[

time: 61.6 us -> 57.9 us (0.940)
  Pallas kernels: 57.5 us -> 53.8 us
    pallas_call x3, Pallas kernels: 20.9 us -> 17.7 us  [local(): pl.pallas_call(functools.partial(update_kernel, batch, per_block, members...]
where the time goes in v3:
time: 57.9 us; the launch traced here: 57.8 us
  Pallas kernels  53.8 us (93%)
  local copies, waits for them, and re-layouts  3.85 us (7%)
    pallas_call x2, Pallas kernels, exchange(): pl.pallas_call(functools.partial(exchange_kernel, digits, cap, width), ou...  21.4 us
    pallas_call x3, Pallas kernels, local(): pl.pallas_call(functools.partial(update_kernel, batch, per_block, members...  17.7 us
    pallas_call x1, Pallas kernels, local(): pl.pallas_call(functools.partial(first_kernel, digits, cap, capp, aug, pe...  14.1 us
    reshape x1, local copies, waits for them, and re-layouts, local(): state = ensemble.reshape(aug * per_member, LANES)  1.77 us
    reshape x1, local copies, waits for them, and re-layouts, local(): return out.reshape(aug, levels, rows_dev, cols_dev)  1.38 us

profile of v3, /device:TPU:0, one launch (start us, length us, event | category | flops | bytes accessed | tf_op | source)
XLA Modules:
  0.0 57.8 jit_solution(14878291074663436166)
XLA Ops:
  0.0 0.7 %copy.10 = s32[3,64,1,1]{1,0,2,3:T(4,128)S(1)} copy(s32[3,64,1,1]{1,3,2,0:T(1,128)} %param.13) | data formatting | bytes 1536
  0.7 0.0 copy-start.1
  0.7 0.0 copy-start.2
  0.7 0.0 copy-start.3
  0.7 0.0 copy-start.4
  0.7 1.8 %reshape.19.state_ref = f32[1620,128]{1,0:T(8,128)S(1)} reshape(f32[81,10,2,128]{3,2,1,0:T(2,128)} %param.7) | data formatting | bytes 1658880 | tf_op jit(solution)/shard_map/reshape | solution.py:346
  2.5 0.0 copy-done.1
  2.5 0.0 copy-done.2
  2.5 0.0 copy-done.3
  2.5 0.0 copy-done.4
  2.5 0.0 copy-start
  2.5 14.1 %first.1 = (f32[2,2,2,4,32,128]{5,4,3,2,1,0:T(8,128)S(1)}, f32[192,128]{1,0:T(8,128)S(1)}, s32[3,512]{1,0:T(4,128)S(1)}) custom-call(f32[3,512]{1,0:T(4,128)S(1)} %copy-done.1, f32[3,512]{1,0:T(4,128)S(1)} %copy-done.2, s32[3,512]{1,0:T(4,128)S(1)} %copy-done.3, s32[3,512]{1,0:T(4,128)S(1)} %copy-done.4, f32[1620,128]{1,0:T(8,128)S(1)} %reshape.19.state_ref), custom_call_target="tpu_custom_call" | custom-call | tf_op jit(solution)/shard_map/first/pallas_call | solution.py:352
  16.6 0.0 copy-done
  16.6 5.9 %update.3.x_ref = f32[160,128]{1,0:T(8,128)S(1)} custom-call(s32[3,64]{1,0:T(4,128)S(1)} %bitcast.9, s32[3,512]{1,0:T(4,128)S(1)} %copy-done, s32[3,512]{1,0:T(4,128)S(1)} %get-tuple-element.8.pos_ref, f32[192,128]{1,0:T(8,128)S(1)} %get-tuple-element.9.x_ref, f32[1024,128]{1,0:T(8,128)S(1)} %bitcast.8), custom_call_target="tpu_custom_call" | custom-call | tf_op jit(solution)/shard_map/update/pallas_call | solution.py:371
  22.5 11.0 %exchange.2 = f32[2,2,2,4,32,128]{5,4,3,2,1,0:T(8,128)S(1)} custom-call(f32[160,128]{1,0:T(8,128)S(1)} %update.3.x_ref), custom_call_target="tpu_custom_call" | custom-call | tf_op jit(solution)/shard_map/exchange/pallas_call | solution.py:158
  33.5 5.9 %update.4.x_ref = f32[128,128]{1,0:T(8,128)S(1)} custom-call(s32[3,64]{1,0:T(4,128)S(1)} %bitcast.10, s32[3,512]{1,0:T(4,128)S(1)} %copy-done, s32[3,512]{1,0:T(4,128)S(1)} %get-tuple-element.8.pos_ref, f32[160,128]{1,0:T(8,128)S(1)} %update.3.x_ref, f32[1024,128]{1,0:T(8,128)S(1)} %bitcast.7), custom_call_target="tpu_custom_call" | custom-call | tf_op jit(solution)/shard_map/update/pallas_call | solution.py:371
  39.5 10.4 %exchange.3 = f32[2,2,2,4,32,128]{5,4,3,2,1,0:T(8,128)S(1)} custom-call(f32[128,128]{1,0:T(8,128)S(1)} %update.4.x_ref), custom_call_target="tpu_custom_call" | custom-call | tf_op jit(solution)/shard_map/exchange/pallas_call | solution.py:158
  49.9 5.9 %update.5.x_ref = f32[96,128]{1,0:T(8,128)S(1)} custom-call(s32[3,64]{1,0:T(4,128)S(1)} %bitcast.11, s32[3,512]{1,0:T(4,128)S(1)} %copy-done, s32[3,512]{1,0:T(4,128)S(1)} %get-tuple-element.8.pos_ref, f32[128,128]{1,0:T(8,128)S(1)} %update.4.x_ref, f32[1024,128]{1,0:T(8,128)S(1)} %bitcast.6), custom_call_target="tpu_custom_call" | custom-call | tf_op jit(solution)/shard_map/update/pallas_call | solution.py:371
  55.8 0.6 %final.1 = f32[1620,128]{1,0:T(8,128)S(1)} custom-call(f32[96,128]{1,0:T(8,128)S(1)} %update.5.x_ref, f32[1620,128]{1,0:T(8,128)S(1)} %reshape.19.state_ref), custom_call_target="tpu_custom_call" | custom-call | tf_op jit(solution)/shard_map/final/pallas_call | solution.py:384
  56.4 1.4 %reshape.23 = f32[81,10,2,128]{3,2,1,0:T(2,128)} reshape(f32[1620,128]{1,0:T(8,128)S(1)} %final.1) | data formatting | bytes 1658880 | tf_op jit(solution)/shard_map/reshape | solution.py:392
Async XLA Ops:
  0.7 1.8 %copy-start.1 = (f32[3,512]{1,0:T(4,128)S(1)}, f32[3,512]{1,0:T(4,128)}, u32[]{:S(2)}) copy-start(f32[3,512]{1,0:T(4,128)} %values_ref.1) | copy-start | bytes 18436
  0.7 1.8 %copy-start.2 = (f32[3,512]{1,0:T(4,128)S(1)}, f32[3,512]{1,0:T(4,128)}, u32[]{:S(2)}) copy-start(f32[3,512]{1,0:T(4,128)} %errors_ref.1) | copy-start | bytes 18436
  0.7 1.8 %copy-start.3 = (s32[3,512]{1,0:T(4,128)S(1)}, s32[3,512]{1,0:T(4,128)}, u32[]{:S(2)}) copy-start(s32[3,512]{1,0:T(4,128)} %device_ref.1) | copy-start | bytes 18436
  0.7 1.8 %copy-start.4 = (s32[3,512]{1,0:T(4,128)S(1)}, s32[3,512]{1,0:T(4,128)}, u32[]{:S(2)}) copy-start(s32[3,512]{1,0:T(4,128)} %cell_ref.1) | copy-start | bytes 18436
  2.5 14.1 %copy-start = (s32[3,512]{1,0:T(4,128)S(1)}, s32[3,512]{1,0:T(4,128)}, u32[]{:S(2)}) copy-start(s32[3,512]{1,0:T(4,128)} %order_ref.5) | copy-start | bytes 18436

commit v4 on v3

--- a/solution.py
+++ b/solution.py
@@ -10,6 +10,7 @@
 MESH = pl.DeviceIdType.MESH
 GROUP = 32
 LANES = 128
+PLANE = ((0, 0), (1, 0), (0, 1), (1, 1))
 VMEM_LIMIT = 32 * 1024 * 1024
 
 
@@ -65,8 +66,9 @@
 
     grid = [size for _, _, size in digits] == [4, 2, 2, 2]
     partners = [((which, step),) for which, (_, _, size) in enumerate(digits) for step in range(1, size)]
+    spread = [(dz, turn) for dz in (2, 1, 3, 0) for turn in PLANE[::-1] if dz or any(turn)]
     if grid:
-        partners.append(((1, 1), (2, 1)))
+        partners = [((0, dz), (1, dx), (2, dy)) for dz, (dx, dy) in spread] + [((3, 1),)]
     barrier = pltpu.get_barrier_semaphore()
     for moves in partners:
         pl.semaphore_signal(barrier, inc=1, device_id=peer(*moves), device_id_type=MESH)
@@ -102,21 +104,16 @@
 
     if grid:
         z, x, y, k = mine
-        plane = [peer((1, 1)), peer((2, 1)), peer((1, 1), (2, 1))]
         other = peer((3, 1))
-        line = [(step, send((k, y, x, z), peer((0, step)))) for step in (1, 3, 2)]
-        arriving = [[send((k, y, x, z), device)] for device in plane]
+        arriving = {turn: [] for turn in PLANE}
+        for dz, (dx, dy) in spread:
+            arriving[dx, dy].append(send((k, y, x, z), peer((0, dz), (1, dx), (2, dy))))
         meanwhile()
-        for step, copy in line:
-            copy.wait_recv()
-            chunk = lax.rem(z + 4 - step, 4)
-            for place_now, device in enumerate(plane):
-                arriving[place_now].append(send((k, y, x, chunk), device))
-        last = [send((k, y, x), other)]
-        for copies, (yy, xx) in zip(arriving, ((y, 1 - x), (1 - y, x), (1 - y, 1 - x))):
-            for copy in copies:
+        last = []
+        for dx, dy in PLANE:
+            for copy in arriving[dx, dy]:
                 copy.wait_recv()
-            last.append(send((k, yy, xx), other))
+            last.append(send((k, lax.rem(y + dy, 2), lax.rem(x + dx, 2)), other))
         for copy in last:
             copy.wait_recv()
     else:

time: 57.9 us -> 56.9 us (0.983)
  Pallas kernels: 53.8 us -> 52.8 us
    pallas_call x1, Pallas kernels: 14.1 us -> 12.8 us  [local(): pl.pallas_call(functools.partial(first_kernel, digits, cap, capp, aug, pe...]
where the time goes in v4:
time: 56.9 us; the launch traced here: 56.7 us
  Pallas kernels  52.8 us (93%)
  local copies, waits for them, and re-layouts  3.85 us (7%)
    pallas_call x2, Pallas kernels, exchange(): pl.pallas_call(functools.partial(exchange_kernel, digits, cap, width), ou...  21.6 us
    pallas_call x3, Pallas kernels, local(): pl.pallas_call(functools.partial(update_kernel, batch, per_block, members...  17.7 us
    pallas_call x1, Pallas kernels, local(): pl.pallas_call(functools.partial(first_kernel, digits, cap, capp, aug, pe...  12.8 us
    reshape x1, local copies, waits for them, and re-layouts, local(): state = ensemble.reshape(aug * per_member, LANES)  1.77 us
    reshape x1, local copies, waits for them, and re-layouts, local(): return out.reshape(aug, levels, rows_dev, cols_dev)  1.38 us

profile of v4, /device:TPU:0, one launch (start us, length us, event | category | flops | bytes accessed | tf_op | source)
XLA Modules:
  0.0 56.7 jit_solution(5222962399257200466)
XLA Ops:
  0.0 0.7 %copy.10 = s32[3,64,1,1]{1,0,2,3:T(4,128)S(1)} copy(s32[3,64,1,1]{1,3,2,0:T(1,128)} %param.13) | data formatting | bytes 1536
  0.7 0.0 copy-start.1
  0.7 0.0 copy-start.2
  0.7 0.0 copy-start.3
  0.7 0.0 copy-start.4
  0.7 1.8 %reshape.19.state_ref = f32[1620,128]{1,0:T(8,128)S(1)} reshape(f32[81,10,2,128]{3,2,1,0:T(2,128)} %param.7) | data formatting | bytes 1658880 | tf_op jit(solution)/shard_map/reshape | solution.py:343
  2.5 0.0 copy-done.1
  2.5 0.0 copy-done.2
  2.5 0.0 copy-done.3
  2.5 0.0 copy-done.4
  2.5 0.0 copy-start
  2.5 12.8 %first.1 = (f32[2,2,2,4,32,128]{5,4,3,2,1,0:T(8,128)S(1)}, f32[192,128]{1,0:T(8,128)S(1)}, s32[3,512]{1,0:T(4,128)S(1)}) custom-call(f32[3,512]{1,0:T(4,128)S(1)} %copy-done.1, f32[3,512]{1,0:T(4,128)S(1)} %copy-done.2, s32[3,512]{1,0:T(4,128)S(1)} %copy-done.3, s32[3,512]{1,0:T(4,128)S(1)} %copy-done.4, f32[1620,128]{1,0:T(8,128)S(1)} %reshape.19.state_ref), custom_call_target="tpu_custom_call" | custom-call | tf_op jit(solution)/shard_map/first/pallas_call | solution.py:349
  15.3 0.0 copy-done
  15.4 5.9 %update.3.x_ref = f32[160,128]{1,0:T(8,128)S(1)} custom-call(s32[3,64]{1,0:T(4,128)S(1)} %bitcast.9, s32[3,512]{1,0:T(4,128)S(1)} %copy-done, s32[3,512]{1,0:T(4,128)S(1)} %get-tuple-element.8.pos_ref, f32[192,128]{1,0:T(8,128)S(1)} %get-tuple-element.9.x_ref, f32[1024,128]{1,0:T(8,128)S(1)} %bitcast.8), custom_call_target="tpu_custom_call" | custom-call | tf_op jit(solution)/shard_map/update/pallas_call | solution.py:368
  21.2 10.9 %exchange.2 = f32[2,2,2,4,32,128]{5,4,3,2,1,0:T(8,128)S(1)} custom-call(f32[160,128]{1,0:T(8,128)S(1)} %update.3.x_ref), custom_call_target="tpu_custom_call" | custom-call | tf_op jit(solution)/shard_map/exchange/pallas_call | solution.py:155
  32.1 5.9 %update.4.x_ref = f32[128,128]{1,0:T(8,128)S(1)} custom-call(s32[3,64]{1,0:T(4,128)S(1)} %bitcast.10, s32[3,512]{1,0:T(4,128)S(1)} %copy-done, s32[3,512]{1,0:T(4,128)S(1)} %get-tuple-element.8.pos_ref, f32[160,128]{1,0:T(8,128)S(1)} %update.3.x_ref, f32[1024,128]{1,0:T(8,128)S(1)} %bitcast.7), custom_call_target="tpu_custom_call" | custom-call | tf_op jit(solution)/shard_map/update/pallas_call | solution.py:368
  38.0 10.8 %exchange.3 = f32[2,2,2,4,32,128]{5,4,3,2,1,0:T(8,128)S(1)} custom-call(f32[128,128]{1,0:T(8,128)S(1)} %update.4.x_ref), custom_call_target="tpu_custom_call" | custom-call | tf_op jit(solution)/shard_map/exchange/pallas_call | solution.py:155
  48.8 5.9 %update.5.x_ref = f32[96,128]{1,0:T(8,128)S(1)} custom-call(s32[3,64]{1,0:T(4,128)S(1)} %bitcast.11, s32[3,512]{1,0:T(4,128)S(1)} %copy-done, s32[3,512]{1,0:T(4,128)S(1)} %get-tuple-element.8.pos_ref, f32[128,128]{1,0:T(8,128)S(1)} %update.4.x_ref, f32[1024,128]{1,0:T(8,128)S(1)} %bitcast.6), custom_call_target="tpu_custom_call" | custom-call | tf_op jit(solution)/shard_map/update/pallas_call | solution.py:368
  54.7 0.6 %final.1 = f32[1620,128]{1,0:T(8,128)S(1)} custom-call(f32[96,128]{1,0:T(8,128)S(1)} %update.5.x_ref, f32[1620,128]{1,0:T(8,128)S(1)} %reshape.19.state_ref), custom_call_target="tpu_custom_call" | custom-call | tf_op jit(solution)/shard_map/final/pallas_call | solution.py:381
  55.3 1.4 %reshape.23 = f32[81,10,2,128]{3,2,1,0:T(2,128)} reshape(f32[1620,128]{1,0:T(8,128)S(1)} %final.1) | data formatting | bytes 1658880 | tf_op jit(solution)/shard_map/reshape | solution.py:389
Async XLA Ops:
  0.7 1.8 %copy-start.1 = (f32[3,512]{1,0:T(4,128)S(1)}, f32[3,512]{1,0:T(4,128)}, u32[]{:S(2)}) copy-start(f32[3,512]{1,0:T(4,128)} %values_ref.1) | copy-start | bytes 18436
  0.7 1.8 %copy-start.2 = (f32[3,512]{1,0:T(4,128)S(1)}, f32[3,512]{1,0:T(4,128)}, u32[]{:S(2)}) copy-start(f32[3,512]{1,0:T(4,128)} %errors_ref.1) | copy-start | bytes 18436
  0.7 1.8 %copy-start.3 = (s32[3,512]{1,0:T(4,128)S(1)}, s32[3,512]{1,0:T(4,128)}, u32[]{:S(2)}) copy-start(s32[3,512]{1,0:T(4,128)} %device_ref.1) | copy-start | bytes 18436
  0.7 1.8 %copy-start.4 = (s32[3,512]{1,0:T(4,128)S(1)}, s32[3,512]{1,0:T(4,128)}, u32[]{:S(2)}) copy-start(s32[3,512]{1,0:T(4,128)} %cell_ref.1) | copy-start | bytes 18436
  2.5 12.8 %copy-start = (s32[3,512]{1,0:T(4,128)S(1)}, s32[3,512]{1,0:T(4,128)}, u32[]{:S(2)}) copy-start(s32[3,512]{1,0:T(4,128)} %order_ref.5) | copy-start | bytes 18436

commit v5 on v4

--- a/solution.py
+++ b/solution.py
@@ -1,5 +1,4 @@
 import functools
-import itertools
 import jax
 import jax.numpy as jnp
 from jax import lax
@@ -52,109 +51,125 @@
     return 24 if cap == 32 and LANES - width >= (width + 1) // 2 else cap
 
 
-def exchange_body(digits, cap, width, fill, meanwhile, buf_ref, send_sem, recv_sem):
-    place = {axis: lax.axis_index(axis) for axis in ("lat", "lon")}
-    mine = [lax.rem(place[axis] // stride, size) for axis, stride, size in digits]
-
-    def peer(*moves):
-        moved = dict(place)
+def is_grid(digits):
+    return [size for _, _, size in digits] == [4, 2, 2, 2]
+
+
+class Exchange:
+    def __init__(self, digits, cap, width):
+        self.digits, self.cap, self.width = digits, cap, width
+        self.sent = fold_of(cap, width)
+        self.place = {axis: lax.axis_index(axis) for axis in ("lat", "lon")}
+        self.mine = [lax.rem(self.place[axis] // stride, size) for axis, stride, size in digits]
+        self.weights = [1]
+        for _, _, size in digits:
+            self.weights.append(self.weights[-1] * size)
+        if is_grid(digits):
+            self.spread = [(dz, turn) for dz in (2, 1, 3, 0) for turn in PLANE[::-1] if dz or any(turn)]
+            self.partners = [((0, dz), (1, dx), (2, dy)) for dz, (dx, dy) in self.spread] + [((3, 1),)]
+        else:
+            self.partners = [
+                ((which, step),) for which, (_, _, size) in enumerate(digits) for step in range(1, size)
+            ]
+
+    def peer(self, *moves):
+        moved = dict(self.place)
         for which, step in moves:
-            axis, stride, size = digits[which]
-            other = lax.rem(mine[which] + step, size)
-            moved[axis] = moved[axis] + (other - mine[which]) * stride
+            axis, stride, size = self.digits[which]
+            other = lax.rem(self.mine[which] + step, size)
+            moved[axis] = moved[axis] + (other - self.mine[which]) * stride
         return (moved["lat"], moved["lon"])
 
-    grid = [size for _, _, size in digits] == [4, 2, 2, 2]
-    partners = [((which, step),) for which, (_, _, size) in enumerate(digits) for step in range(1, size)]
-    spread = [(dz, turn) for dz in (2, 1, 3, 0) for turn in PLANE[::-1] if dz or any(turn)]
-    if grid:
-        partners = [((0, dz), (1, dx), (2, dy)) for dz, (dx, dy) in spread] + [((3, 1),)]
-    barrier = pltpu.get_barrier_semaphore()
-    for moves in partners:
-        pl.semaphore_signal(barrier, inc=1, device_id=peer(*moves), device_id_type=MESH)
-    own = tuple(mine[::-1])
-    sent = fold_of(cap, width)
-    half = (width + 1) // 2
-    chunk_now = fill()
-    if sent < cap:
-        tail = chunk_now[24:32]
-        lane = lax.broadcasted_iota(jnp.int32, tail.shape, 1)
-        low = jnp.where(lane < half, tail, 0.0)
-        high = jnp.where((lane >= half) & (lane < width), tail, 0.0)
-        buf_ref[own + (slice(0, 8),)] = chunk_now[0:8] + pltpu.roll(low, width, 1)
-        buf_ref[own + (slice(8, 16),)] = chunk_now[8:16] + pltpu.roll(high, width - half, 1)
-        buf_ref[own + (slice(16, 24),)] = chunk_now[16:24]
-    else:
-        buf_ref[own] = chunk_now
-    pl.semaphore_wait(barrier, len(partners))
-
-    sends = []
-
-    def send(part, device):
-        slot = len(sends)
-        part = part + (slice(None),) * (len(digits) - len(part)) + (pl.ds(0, sent),)
-        copy = pltpu.make_async_remote_copy(
-            src_ref=buf_ref.at[part], dst_ref=buf_ref.at[part],
-            send_sem=send_sem.at[slot], recv_sem=recv_sem.at[slot],
-            device_id=device, device_id_type=MESH,
-        )
-        copy.start()
-        sends.append(copy)
-        return copy
-
-    if grid:
-        z, x, y, k = mine
-        other = peer((3, 1))
-        arriving = {turn: [] for turn in PLANE}
-        for dz, (dx, dy) in spread:
-            arriving[dx, dy].append(send((k, y, x, z), peer((0, dz), (1, dx), (2, dy))))
-        meanwhile()
-        last = []
-        for dx, dy in PLANE:
-            for copy in arriving[dx, dy]:
+    def greet(self):
+        barrier = pltpu.get_barrier_semaphore()
+        for moves in self.partners:
+            pl.semaphore_signal(barrier, inc=1, device_id=self.peer(*moves), device_id_type=MESH)
+
+    def await_greetings(self):
+        pl.semaphore_wait(pltpu.get_barrier_semaphore(), len(self.partners))
+
+    def place_own(self, chunk, buf_ref):
+        width, sent = self.width, self.sent
+        half = (width + 1) // 2
+        own = sum(digit * weight for digit, weight in zip(self.mine, self.weights))
+        if sent < self.cap:
+            tail = chunk[24:32]
+            lane = lax.broadcasted_iota(jnp.int32, tail.shape, 1)
+            low = jnp.where(lane < half, tail, 0.0)
+            high = jnp.where((lane >= half) & (lane < width), tail, 0.0)
+            buf_ref[own, 0:8] = chunk[0:8] + pltpu.roll(low, width, 1)
+            buf_ref[own, 8:16] = chunk[8:16] + pltpu.roll(high, width - half, 1)
+            buf_ref[own, 16:24] = chunk[16:24]
+        else:
+            buf_ref[own] = chunk
+
+    def run(self, buf_ref, send_sem, recv_sem, meanwhile=lambda: None):
+        digits, mine, weights, sent = self.digits, self.mine, self.weights, self.sent
+        sends = []
+
+        def send(start, count, device):
+            slot = len(sends)
+            part = buf_ref.at[pl.ds(start, count), pl.ds(0, sent)]
+            copy = pltpu.make_async_remote_copy(
+                src_ref=part, dst_ref=part, send_sem=send_sem.at[slot], recv_sem=recv_sem.at[slot],
+                device_id=device, device_id_type=MESH,
+            )
+            copy.start()
+            sends.append(copy)
+            return copy
+
+        if is_grid(digits):
+            z, x, y, k = mine
+            arriving = {turn: [] for turn in PLANE}
+            for dz, (dx, dy) in self.spread:
+                own = z + 4 * x + 8 * y + 16 * k
+                arriving[dx, dy].append(send(own, 1, self.peer((0, dz), (1, dx), (2, dy))))
+            meanwhile()
+            last = []
+            for dx, dy in PLANE:
+                for copy in arriving[dx, dy]:
+                    copy.wait_recv()
+                start = 4 * lax.rem(x + dx, 2) + 8 * lax.rem(y + dy, 2) + 16 * k
+                last.append(send(start, 4, self.peer((3, 1))))
+            for copy in last:
                 copy.wait_recv()
-            last.append(send((k, lax.rem(y + dy, 2), lax.rem(x + dx, 2)), other))
-        for copy in last:
-            copy.wait_recv()
-    else:
-        for which, (_, _, size) in enumerate(digits):
-            part = tuple(mine[which:][::-1])
-            stage = [send(part, peer((which, step))) for step in range(1, size)]
-            if which == 0:
-                meanwhile()
-            for copy in stage:
-                copy.wait_recv()
-    for copy in sends:
-        copy.wait_send()
-    if sent < cap:
-        for spot in itertools.product(*(range(size) for _, _, size in digits[::-1])):
-            low = pltpu.roll(buf_ref[spot + (slice(0, 8),)], LANES - width, 1)
-            high = pltpu.roll(buf_ref[spot + (slice(8, 16),)], LANES - width + half, 1)
-            lane = lax.broadcasted_iota(jnp.int32, low.shape, 1)
-            buf_ref[spot + (slice(24, 32),)] = jnp.where(lane < half, low, high)
+        else:
+            for which, (_, _, size) in enumerate(digits):
+                start = sum(mine[i] * weights[i] for i in range(which, len(digits)))
+                stage = [send(start, weights[which], self.peer((which, step))) for step in range(1, size)]
+                if which == 0:
+                    meanwhile()
+                for copy in stage:
+                    copy.wait_recv()
+        for copy in sends:
+            copy.wait_send()
+        if sent < self.cap:
+            width = self.width
+            half = (width + 1) // 2
+            for spot in range(weights[-1]):
+                low = pltpu.roll(buf_ref[spot, 0:8], LANES - width, 1)
+                high = pltpu.roll(buf_ref[spot, 8:16], LANES - width + half, 1)
+                lane = lax.broadcasted_iota(jnp.int32, low.shape, 1)
+                buf_ref[spot, 24:32] = jnp.where(lane < half, low, high)
 
 
 def exchange_kernel(digits, cap, width, x_ref, buf_ref, send_sem, recv_sem):
-    exchange_body(
-        digits, cap, width, lambda: x_ref[0:cap, :], lambda: None, buf_ref, send_sem, recv_sem
-    )
+    trade = Exchange(digits, cap, width)
+    trade.greet()
+    trade.place_own(x_ref[0:cap, :], buf_ref)
+    trade.await_greetings()
+    trade.run(buf_ref, send_sem, recv_sem)
 
 
 def exchange_scratch(digits):
-    copies = 19 if [s for _, _, s in digits] == [4, 2, 2, 2] else sum(s - 1 for _, _, s in digits)
+    copies = 19 if is_grid(digits) else sum(s - 1 for _, _, s in digits)
     return [pltpu.SemaphoreType.DMA((copies,)), pltpu.SemaphoreType.DMA((copies,))]
 
 
-def buffer_shape(digits, cap):
-    return jax.ShapeDtypeStruct(
-        tuple(size for _, _, size in digits[::-1]) + (cap, LANES), jnp.float32
-    )
-
-
-def exchange(x, digits, cap, width, ident):
+def exchange(x, digits, cap, width, ident, ndev):
     return pl.pallas_call(
         functools.partial(exchange_kernel, digits, cap, width),
-        out_shape=buffer_shape(digits, cap),
+        out_shape=jax.ShapeDtypeStruct((ndev, cap, LANES), jnp.float32),
         in_specs=[vspec()],
         out_specs=vspec(),
         scratch_shapes=exchange_scratch(digits),
@@ -165,8 +180,11 @@
     )(x)
 
 
-def first_kernel(digits, cap, capp, aug, per_member, base, values_ref, errors_ref, device_ref, cell_ref,
-                 state_ref, buf_ref, x_ref, pos_ref, send_sem, recv_sem):
+def first_kernel(digits, cap, capp, aug, per_member, base, per_block, values_ref, errors_ref,
+                 device_ref, cell_ref, order_ref, coupled_ref, state_ref, buf_ref, x_ref, source_ref, count_ref,
+                 send_sem, recv_sem):
+    trade = Exchange(digits, cap, aug + 3)
+    trade.greet()
     nbatch, nobs = device_ref.shape
     n_lat, n_lon = lax.axis_size("lat"), lax.axis_size("lon")
     ndev = n_lat * n_lon
@@ -184,6 +202,7 @@
         slot = lax.broadcasted_iota(jnp.int32, (capp, nobs), 0).astype(jnp.float32)
         lane = lax.broadcasted_iota(jnp.int32, (capp, LANES), 1)
         cells = []
+        most = jnp.max(jnp.sum(coupled_ref[...].astype(jnp.float32), axis=1, keepdims=True), axis=0, keepdims=True)
         for batch in range(nbatch):
             row = slice(batch, batch + 1)
             chosen = (rank[row] == slot) & (owned[row] > 0)
@@ -193,7 +212,9 @@
 
             cells.append(total(cell_ref))
             x_ref[batch * capp:(batch + 1) * capp, :] = jnp.where(
-                lane == aug, total(values_ref), jnp.where(lane == aug + 1, total(errors_ref), 0.0)
+                lane == aug, total(values_ref), jnp.where(
+                    lane == aug + 1, total(errors_ref), jnp.where(lane == aug + 2, most, 0.0)
+                )
             )
         cell = jnp.concatenate(cells, axis=0).astype(jnp.int32)
         wide = 2 * LANES
@@ -219,6 +240,8 @@
             lax.broadcasted_iota(jnp.int32, square, 0) == lax.broadcasted_iota(jnp.int32, square, 1)
         ).astype(jnp.float32)
         names = lax.broadcasted_iota(jnp.int32, (ndev, nobs), 0)
+        names_obs = lax.broadcasted_iota(jnp.int32, (nobs, nobs), 0)
+        targets = ranks(coupled_ref[...].astype(jnp.float32))
         for batch in range(nbatch):
             device = device_ref[batch:batch + 1, :]
             held = (device == names).astype(jnp.float32)
@@ -228,9 +251,31 @@
             for axis, stride, size in digits:
                 slab = slab + pow2_part(place[axis], stride, size) * weight
                 weight *= size
-            pos_ref[batch:batch + 1, :] = slab * cap + rank.astype(jnp.int32)
-
-    exchange_body(digits, cap, aug + 2, fill, meanwhile, buf_ref, send_sem, recv_sem)
+            pos = slab * cap + rank.astype(jnp.int32)
+            part = lax.broadcasted_iota(jnp.int32, (8, nobs), 0)
+            parts = jnp.where(part == 0, pos & 63, jnp.where(part == 1, (pos >> 6) & 63, pos >> 12))
+            parts = jnp.where(part < 3, parts, 0).astype(jnp.float32).astype(jnp.bfloat16)
+            named = (order_ref[batch:batch + 1, :] == names_obs).astype(jnp.float32).astype(jnp.bfloat16)
+            ordered = jnp.dot(parts, named, preferred_element_type=jnp.float32)
+            goes = (targets[batch:batch + 1, :] == names_obs.astype(jnp.float32)) & (
+                coupled_ref[batch:batch + 1, :] > 0
+            )
+            packed = lax.dot_general(
+                ordered.astype(jnp.bfloat16), goes.astype(jnp.float32).astype(jnp.bfloat16), (NT, ((), ())),
+                preferred_element_type=jnp.float32,
+            ).astype(jnp.int32)
+            source_ref[batch:batch + 1, :] = packed[0:1] + 64 * packed[1:2] + 4096 * packed[2:3]
+            count_ref[batch] = jnp.sum(coupled_ref[batch:batch + 1, :]) // per_block
+
+    trade.place_own(fill(), buf_ref)
+    trade.await_greetings()
+    trade.run(buf_ref, send_sem, recv_sem, meanwhile)
+    most = buf_ref[0, 0:1]
+    for spot in range(1, ndev):
+        most = jnp.maximum(most, buf_ref[spot, 0:1])
+    lane = lax.broadcasted_iota(jnp.int32, (1, LANES), 1)
+    most = jnp.max(jnp.where(lane == aug + 2, most, 0.0))
+    count_ref[nbatch] = most.astype(jnp.int32) // per_block
 
 
 def group_update(z, valid, x, per_block, members):
@@ -284,29 +329,49 @@
     return x + (mm3(first, v_half[0]) + mm3(second, v_half[1]))
 
 
-def update_kernel(batch, per_block, members, capp, coupled_ref, order_ref, pos_ref, x_ref, buf_ref, out_ref, z_ref, list_ref):
+def gather_rows(read, source_ref, batch, start, per_block, z_ref):
+    @pl.loop(0, GROUP, unroll=8)
+    def _(b):
+        for i in range(per_block):
+            z_ref[pl.ds(i * GROUP + b, 1), :] = read(source_ref[batch, (start + b) * per_block + i])
+
+
+def group_of(z_ref, total, start, x, per_block, members):
+    valid = (start + lax.broadcasted_iota(jnp.int32, (GROUP, 1), 0) < total).astype(jnp.float32)
+    z = [z_ref[i * GROUP:(i + 1) * GROUP, :] for i in range(per_block)]
+    return group_update(z, valid, x, per_block, members)
+
+
+def update_kernel(batch, per_block, members, capp, source_ref, count_ref, x_ref, buf_ref, out_ref, z_ref):
     out_ref[...] = x_ref[capp:, :]
-    total = jnp.int32(0)
-    for block in range(coupled_ref.shape[1]):
-        list_ref[total] = block
-        total = total + (coupled_ref[batch, block] > 0).astype(jnp.int32)
+    total = count_ref[batch]
 
     @pl.loop(0, (total + GROUP - 1) // GROUP)
     def _(group):
         start = group * GROUP
-
-        @pl.loop(0, GROUP, unroll=8)
-        def _(b):
-            block = list_ref[jnp.minimum(start + b, total - 1)]
-            for i in range(per_block):
-                source = pos_ref[batch, order_ref[batch, block * per_block + i]]
-                z_ref[pl.ds(i * GROUP + b, 1), :] = buf_ref[pl.ds(source, 1), :]
-
-        valid = (
-            start + lax.broadcasted_iota(jnp.int32, (GROUP, 1), 0) < total
-        ).astype(jnp.float32)
-        z = [z_ref[i * GROUP:(i + 1) * GROUP, :] for i in range(per_block)]
-        out_ref[...] = group_update(z, valid, out_ref[...], per_block, members)
+        gather_rows(lambda row: buf_ref[pl.ds(row, 1), :], source_ref, batch, start, per_block, z_ref)
+        out_ref[...] = group_of(z_ref, total, start, out_ref[...], per_block, members)
+
+
+def rest_kernel(digits, cap, width, per_block, members, source_ref, count_ref, x_ref, buf_ref, out_ref, z_ref, *more):
+    nbatch = len(more) // 3 + 1
+    trade = Exchange(digits, cap, width)
+    trade.greet()
+    shift = cap.bit_length() - 1
+    x = x_ref[...]
+    for batch in range(nbatch):
+        def read(row, held=buf_ref):
+            return held[row >> shift, pl.ds(row & (cap - 1), 1), :]
+
+        gather_rows(read, source_ref, batch, 0, per_block, z_ref)
+        x = group_of(z_ref, count_ref[batch], 0, x[cap:], per_block, members)
+        if batch == 0:
+            trade.await_greetings()
+        if batch + 1 < nbatch:
+            buf_ref, send_sem, recv_sem = more[3 * batch:3 * batch + 3]
+            trade.place_own(x[0:cap], buf_ref)
+            trade.run(buf_ref, send_sem, recv_sem)
+    out_ref[...] = x
 
 
 def final_kernel(aug, per_member, x_ref, state_ref, out_ref):
@@ -343,40 +408,61 @@
     state = ensemble.reshape(aug * per_member, LANES)
     params = pltpu.CompilerParams(vmem_limit_bytes=VMEM_LIMIT)
 
-    coupled = coupling.reshape(nbatch, nblocks)
+    coupled = jnp.repeat(coupling.reshape(nbatch, nblocks), per_block, axis=1)
     base = nbatch * capp
     rows = base + -(-aug // 16) * 16
-    buf, x, pos = pl.pallas_call(
-        functools.partial(first_kernel, digits, cap, capp, aug, per_member, base),
+    width = aug + 3
+    buf, x, source, count = pl.pallas_call(
+        functools.partial(first_kernel, digits, cap, capp, aug, per_member, base, per_block),
         out_shape=(
-            buffer_shape(digits, cap),
+            jax.ShapeDtypeStruct((ndev, cap, LANES), jnp.float32),
             jax.ShapeDtypeStruct((rows, LANES), jnp.float32),
             jax.ShapeDtypeStruct((nbatch, nobs), jnp.int32),
+            jax.ShapeDtypeStruct((nbatch + 1,), jnp.int32),
         ),
-        in_specs=[vspec()] * 5,
-        out_specs=(vspec(),) * 3,
+        in_specs=[vspec()] * 7,
+        out_specs=(vspec(), vspec(), vspec(), sspec()),
         scratch_shapes=exchange_scratch(digits),
         compiler_params=pltpu.CompilerParams(
             collective_id=0, has_side_effects=True, vmem_limit_bytes=VMEM_LIMIT
         ),
         name="first",
-    )(obs_values, obs_errors, obs_device, obs_cell, state)
-
-    for batch in range(nbatch):
-        if batch > 0:
-            buf = exchange(x, digits, cap, aug + 2, batch)
-        x = pl.pallas_call(
-            functools.partial(update_kernel, batch, per_block, members, capp),
-            out_shape=jax.ShapeDtypeStruct((rows - (batch + 1) * capp, LANES), jnp.float32),
-            in_specs=[sspec(), sspec(), sspec(), vspec(), vspec()],
+    )(obs_values, obs_errors, obs_device, obs_cell, obs_order, coupled, state)
+    z_scratch = pltpu.VMEM((per_block * GROUP, LANES), jnp.float32)
+
+    def stepwise(x, buf, source, count):
+        for batch in range(nbatch):
+            if batch > 0:
+                buf = exchange(x, digits, cap, width, batch, ndev)
+            x = pl.pallas_call(
+                functools.partial(update_kernel, batch, per_block, members, capp),
+                out_shape=jax.ShapeDtypeStruct((rows - (batch + 1) * capp, LANES), jnp.float32),
+                in_specs=[sspec(), sspec(), vspec(), vspec()],
+                out_specs=vspec(),
+                scratch_shapes=[z_scratch],
+                compiler_params=params,
+                name="update",
+            )(source, count, x, buf.reshape(ndev * cap, LANES))
+        return x
+
+    def together(x, buf, source, count):
+        step_scratch = [pltpu.VMEM((ndev, cap, LANES), jnp.float32)] + exchange_scratch(digits)
+        return pl.pallas_call(
+            functools.partial(rest_kernel, digits, cap, width, per_block, members),
+            out_shape=jax.ShapeDtypeStruct((rows - base, LANES), jnp.float32),
+            in_specs=[sspec(), sspec(), vspec(), vspec()],
             out_specs=vspec(),
-            scratch_shapes=[
-                pltpu.VMEM((per_block * GROUP, LANES), jnp.float32),
-                pltpu.SMEM((nblocks + 1,), jnp.int32),
-            ],
-            compiler_params=params,
-            name="update",
-        )(coupled, obs_order, pos, x, buf.reshape(ndev * cap, LANES))
+            scratch_shapes=[z_scratch] + step_scratch * (nbatch - 1),
+            compiler_params=pltpu.CompilerParams(
+                collective_id=nbatch, has_side_effects=True, vmem_limit_bytes=VMEM_LIMIT
+            ),
+            name="rest",
+        )(source, count, x, buf)
+
+    if is_grid(digits) and cap == capp:
+        x = lax.cond(count[nbatch] <= GROUP, together, stepwise, x, buf, source, count)
+    else:
+        x = stepwise(x, buf, source, count)
 
     out = pl.pallas_call(
         functools.partial(final_kernel, aug, per_member),

time: 56.9 us -> 51 us (0.90)
  Pallas kernels: 52.8 us -> 45.3 us
  local copies, waits for them, and re-layouts: 3.85 us -> 4.61 us
  between operations: 0.11 us -> 0.77 us
    pallas_call x5 -> x1, Pallas kernels: 39.3 us -> 31.2 us  [together(): pl.pallas_call(functools.partial(rest_kernel, digits, cap, width, per_blo...]
    pallas_call x1, Pallas kernels: 12.8 us -> 13.4 us  [local(): pl.pallas_call(functools.partial(first_kernel, digits, cap, capp, aug, pe...]
    slice x0 -> x1, local copies, waits for them, and re-layouts: none -> 0.58 us  [local(): count[nbatch] <= GROUP]
where the time goes in v5:
time: 51 us; the launch traced here: 50.9 us
  Pallas kernels  45.3 us (89%)
  local copies, waits for them, and re-layouts  4.61 us (9%)
  between operations  0.77 us (2%)
    pallas_call x1, Pallas kernels, together(): pl.pallas_call(functools.partial(rest_kernel, digits, cap, width, per_blo...  31.2 us
    pallas_call x1, Pallas kernels, local(): pl.pallas_call(functools.partial(first_kernel, digits, cap, capp, aug, pe...  13.4 us
    reshape x1, local copies, waits for them, and re-layouts, local(): state = ensemble.reshape(aug * per_member, LANES)  1.74 us
    reshape x1, local copies, waits for them, and re-layouts, local(): return out.reshape(aug, levels, rows_dev, cols_dev)  1.38 us

profile of v5, /device:TPU:0, one launch (start us, length us, event | category | flops | bytes accessed | tf_op | source)
XLA Modules:
  0.0 50.9 jit_solution(676442683304292020)
XLA Ops:
  0.0 0.7 %copy.10 = s32[3,64,1,1]{1,0,2,3:T(4,128)S(1)} copy(s32[3,64,1,1]{1,3,2,0:T(1,128)} %param.15) | data formatting | bytes 1536
  0.7 0.1 broadcast_in_dim.3
  0.8 0.1 reshape.26.coupled_ref
  0.9 0.0 copy-start
  0.9 0.0 copy-start.1
  0.9 0.0 copy-start.2
  0.9 0.0 copy-start.3
  0.9 0.0 copy-start.4
  1.0 1.7 %reshape.27.state_ref = f32[1620,128]{1,0:T(8,128)S(1)} reshape(f32[81,10,2,128]{3,2,1,0:T(2,128)} %param.9) | data formatting | bytes 1658880 | tf_op jit(solution)/shard_map/reshape | solution.py:408
  2.7 0.0 copy-done
  2.7 0.0 copy-done.1
  2.7 0.0 copy-done.2
  2.7 0.0 copy-done.3
  2.7 0.0 copy-done.4
  2.7 13.4 %first.1 = (f32[32,32,128]{2,1,0:T(8,128)S(1)}, f32[192,128]{1,0:T(8,128)S(1)}, s32[3,512]{1,0:T(4,128)S(1)}, s32[4]{0:T(128)S(1)}) custom-call(f32[3,512]{1,0:T(4,128)S(1)} %copy-done, f32[3,512]{1,0:T(4,128)S(1)} %copy-done.1, s32[3,512]{1,0:T(4,128)S(1)} %copy-done.2, s32[3,512]{1,0:T(4,128)S(1)} %copy-done.3, s32[3,512]{1,0:T(4,128)S(1)} %copy-done.4, ...), custom_call_target="tpu_custom_call" | custom-call | tf_op jit(solution)/shard_map/first/pallas_call | solution.py:415
  16.2 0.6 %slice.3 = s32[1]{0:T(128)} slice(s32[4]{0:T(128)S(1)} %get-tuple-element.36), slice={[3:4]} | slice | bytes 8 | tf_op jit(solution)/shard_map/slice | solution.py:463
  17.4 31.4 %conditional.1 = (f32[96,128]{1,0:T(8,128)S(1)}) conditional(s32[]{:T(128)} %bitcast.3, (f32[32,32,128]{2,1,0:T(8,128)S(1)}, s32[3,512]{1,0:T(4,128)S(1)}, s32[4]{0:T(128)S(1)}, f32[192,128]{1,0:T(8,128)S(1)}) %tuple.11, (s32[3,512]{1,0:T(4,128)S(1)}, s32[4]{0:T(128)S(1)}, f32[192,128]{1,0:T(8,128)S(1)}, f32[32,32,128]{2,1,0:T(8,128)S(1)}) %tuple.12), branch_computations={%region_0.0_spmd, %region_1.0_spmd} | conditional | bytes 8 | solution.py:463
  17.6 31.2 %rest.1 = f32[96,128]{1,0:T(8,128)S(1)} custom-call(s32[3,512]{1,0:T(4,128)S(1)} %get-tuple-element.28.source_ref, s32[4]{0:T(128)S(1)} %get-tuple-element.29.count_ref, f32[192,128]{1,0:T(8,128)S(1)} %get-tuple-element.30.x_ref, f32[32,32,128]{2,1,0:T(8,128)S(1)} %get-tuple-element.31.buf_ref), custom_call_target="tpu_custom_call" | custom-call | tf_op jit(solution)/shard_map/cond/branch_1_fun/rest/pallas_call | solution.py:450
  48.9 0.6 %final.1 = f32[1620,128]{1,0:T(8,128)S(1)} custom-call(f32[96,128]{1,0:T(8,128)S(1)} %get-tuple-element.40.x_ref, f32[1620,128]{1,0:T(8,128)S(1)} %reshape.27.state_ref), custom_call_target="tpu_custom_call" | custom-call | tf_op jit(solution)/shard_map/final/pallas_call | solution.py:467
  49.5 1.4 %reshape.28 = f32[81,10,2,128]{3,2,1,0:T(2,128)} reshape(f32[1620,128]{1,0:T(8,128)S(1)} %final.1) | data formatting | bytes 1658880 | tf_op jit(solution)/shard_map/reshape | solution.py:475
Async XLA Ops:
  0.9 1.8 %copy-start = (f32[3,512]{1,0:T(4,128)S(1)}, f32[3,512]{1,0:T(4,128)}, u32[]{:S(2)}) copy-start(f32[3,512]{1,0:T(4,128)} %values_ref.1) | copy-start | bytes 18436
  0.9 1.8 %copy-start.1 = (f32[3,512]{1,0:T(4,128)S(1)}, f32[3,512]{1,0:T(4,128)}, u32[]{:S(2)}) copy-start(f32[3,512]{1,0:T(4,128)} %errors_ref.1) | copy-start | bytes 18436
  0.9 1.8 %copy-start.2 = (s32[3,512]{1,0:T(4,128)S(1)}, s32[3,512]{1,0:T(4,128)}, u32[]{:S(2)}) copy-start(s32[3,512]{1,0:T(4,128)} %device_ref.1) | copy-start | bytes 18436
  0.9 1.8 %copy-start.3 = (s32[3,512]{1,0:T(4,128)S(1)}, s32[3,512]{1,0:T(4,128)}, u32[]{:S(2)}) copy-start(s32[3,512]{1,0:T(4,128)} %cell_ref.1) | copy-start | bytes 18436
  0.9 1.8 %copy-start.4 = (s32[3,512]{1,0:T(4,128)S(1)}, s32[3,512]{1,0:T(4,128)}, u32[]{:S(2)}) copy-start(s32[3,512]{1,0:T(4,128)} %order_ref.1) | copy-start | bytes 18436

commit v6 on v5

--- a/solution.py
+++ b/solution.py
@@ -49,6 +49,15 @@
 
 def fold_of(cap, width):
     return 24 if cap == 32 and LANES - width >= (width + 1) // 2 else cap
+
+
+def buffer_rows(ndev, cap):
+    return ndev * cap
+
+
+def row_of(slab, slot, ndev, cap, width):
+    sent = fold_of(cap, width)
+    return jnp.where(slot < sent, slab * sent + slot, ndev * sent + slab * (cap - sent) + slot - sent)
 
 
 def is_grid(digits):
@@ -91,17 +100,18 @@
     def place_own(self, chunk, buf_ref):
         width, sent = self.width, self.sent
         half = (width + 1) // 2
-        own = sum(digit * weight for digit, weight in zip(self.mine, self.weights))
+        own = sum(digit * weight for digit, weight in zip(self.mine, self.weights)) * sent
         if sent < self.cap:
             tail = chunk[24:32]
             lane = lax.broadcasted_iota(jnp.int32, tail.shape, 1)
             low = jnp.where(lane < half, tail, 0.0)
             high = jnp.where((lane >= half) & (lane < width), tail, 0.0)
-            buf_ref[own, 0:8] = chunk[0:8] + pltpu.roll(low, width, 1)
-            buf_ref[own, 8:16] = chunk[8:16] + pltpu.roll(high, width - half, 1)
-            buf_ref[own, 16:24] = chunk[16:24]
+            buf_ref[pl.ds(pl.multiple_of(own, 8), 24), :] = jnp.concatenate(
+                [chunk[0:8] + pltpu.roll(low, width, 1), chunk[8:16] + pltpu.roll(high, width - half, 1), chunk[16:24]],
+                axis=0,
+            )
         else:
-            buf_ref[own] = chunk
+            buf_ref[pl.ds(pl.multiple_of(own, 8), sent), :] = chunk
 
     def run(self, buf_ref, send_sem, recv_sem, meanwhile=lambda: None):
         digits, mine, weights, sent = self.digits, self.mine, self.weights, self.sent
@@ -109,7 +119,7 @@
 
         def send(start, count, device):
             slot = len(sends)
-            part = buf_ref.at[pl.ds(start, count), pl.ds(0, sent)]
+            part = buf_ref.at[pl.ds(pl.multiple_of(start * sent, 8), count * sent)]
             copy = pltpu.make_async_remote_copy(
                 src_ref=part, dst_ref=part, send_sem=send_sem.at[slot], recv_sem=recv_sem.at[slot],
                 device_id=device, device_id_type=MESH,
@@ -147,10 +157,12 @@
             width = self.width
             half = (width + 1) // 2
             for spot in range(weights[-1]):
-                low = pltpu.roll(buf_ref[spot, 0:8], LANES - width, 1)
-                high = pltpu.roll(buf_ref[spot, 8:16], LANES - width + half, 1)
+                at = spot * sent
+                low = pltpu.roll(buf_ref[at:at + 8, :], LANES - width, 1)
+                high = pltpu.roll(buf_ref[at + 8:at + 16, :], LANES - width + half, 1)
                 lane = lax.broadcasted_iota(jnp.int32, low.shape, 1)
-                buf_ref[spot, 24:32] = jnp.where(lane < half, low, high)
+                at = weights[-1] * sent + spot * 8
+                buf_ref[at:at + 8, :] = jnp.where(lane < half, low, high)
 
 
 def exchange_kernel(digits, cap, width, x_ref, buf_ref, send_sem, recv_sem):
@@ -169,7 +181,7 @@
 def exchange(x, digits, cap, width, ident, ndev):
     return pl.pallas_call(
         functools.partial(exchange_kernel, digits, cap, width),
-        out_shape=jax.ShapeDtypeStruct((ndev, cap, LANES), jnp.float32),
+        out_shape=jax.ShapeDtypeStruct((buffer_rows(ndev, cap), LANES), jnp.float32),
         in_specs=[vspec()],
         out_specs=vspec(),
         scratch_shapes=exchange_scratch(digits),
@@ -180,10 +192,10 @@
     )(x)
 
 
-def first_kernel(digits, cap, capp, aug, per_member, base, per_block, values_ref, errors_ref,
+def first_kernel(digits, capp, aug, per_member, base, per_block, values_ref, errors_ref,
                  device_ref, cell_ref, order_ref, coupled_ref, state_ref, buf_ref, x_ref, source_ref, count_ref,
-                 send_sem, recv_sem):
-    trade = Exchange(digits, cap, aug + 3)
+                 most_ref, send_sem, recv_sem):
+    trade = Exchange(digits, capp, aug + 3)
     trade.greet()
     nbatch, nobs = device_ref.shape
     n_lat, n_lon = lax.axis_size("lat"), lax.axis_size("lon")
@@ -196,13 +208,18 @@
     def ranks(flags):
         return jnp.dot(flags.astype(jnp.bfloat16), earlier, preferred_element_type=jnp.float32)
 
+    def coupled_of(batch):
+        return (coupled_ref[batch] > 0).astype(jnp.float32)
+
     def fill():
         owned = (device_ref[...] == me).astype(jnp.float32)
         rank = ranks(owned)
         slot = lax.broadcasted_iota(jnp.int32, (capp, nobs), 0).astype(jnp.float32)
         lane = lax.broadcasted_iota(jnp.int32, (capp, LANES), 1)
         cells = []
-        most = jnp.max(jnp.sum(coupled_ref[...].astype(jnp.float32), axis=1, keepdims=True), axis=0, keepdims=True)
+        most = jnp.zeros((1, 1), jnp.float32)
+        for batch in range(nbatch):
+            most = jnp.maximum(most, jnp.sum(coupled_of(batch), axis=1, keepdims=True))
         for batch in range(nbatch):
             row = slice(batch, batch + 1)
             chosen = (rank[row] == slot) & (owned[row] > 0)
@@ -232,7 +249,7 @@
                 )
                 cut = cut - part.astype(jnp.float32)
         x_ref[0:base, 0:aug] = picked
-        return x_ref[0:cap, :]
+        return x_ref[0:capp, :]
 
     def meanwhile():
         square = (x_ref.shape[0] - base, LANES)
@@ -241,7 +258,10 @@
         ).astype(jnp.float32)
         names = lax.broadcasted_iota(jnp.int32, (ndev, nobs), 0)
         names_obs = lax.broadcasted_iota(jnp.int32, (nobs, nobs), 0)
-        targets = ranks(coupled_ref[...].astype(jnp.float32))
+        nblocks = coupled_ref.shape[2]
+        block = lax.broadcasted_iota(jnp.int32, (nblocks, nobs), 0) * per_block
+        member = lax.broadcasted_iota(jnp.int32, (nblocks, nobs), 1)
+        widen = ((member >= block) & (member < block + per_block)).astype(jnp.float32).astype(jnp.bfloat16)
         for batch in range(nbatch):
             device = device_ref[batch:batch + 1, :]
             held = (device == names).astype(jnp.float32)
@@ -251,34 +271,32 @@
             for axis, stride, size in digits:
                 slab = slab + pow2_part(place[axis], stride, size) * weight
                 weight *= size
-            pos = slab * cap + rank.astype(jnp.int32)
+            pos = row_of(slab, rank.astype(jnp.int32), ndev, capp, aug + 3)
             part = lax.broadcasted_iota(jnp.int32, (8, nobs), 0)
             parts = jnp.where(part == 0, pos & 63, jnp.where(part == 1, (pos >> 6) & 63, pos >> 12))
             parts = jnp.where(part < 3, parts, 0).astype(jnp.float32).astype(jnp.bfloat16)
             named = (order_ref[batch:batch + 1, :] == names_obs).astype(jnp.float32).astype(jnp.bfloat16)
             ordered = jnp.dot(parts, named, preferred_element_type=jnp.float32)
-            goes = (targets[batch:batch + 1, :] == names_obs.astype(jnp.float32)) & (
-                coupled_ref[batch:batch + 1, :] > 0
-            )
+            coupled = jnp.dot(coupled_of(batch).astype(jnp.bfloat16), widen, preferred_element_type=jnp.float32)
+            goes = (ranks(coupled) == names_obs.astype(jnp.float32)) & (coupled > 0.5)
             packed = lax.dot_general(
                 ordered.astype(jnp.bfloat16), goes.astype(jnp.float32).astype(jnp.bfloat16), (NT, ((), ())),
                 preferred_element_type=jnp.float32,
             ).astype(jnp.int32)
             source_ref[batch:batch + 1, :] = packed[0:1] + 64 * packed[1:2] + 4096 * packed[2:3]
-            count_ref[batch] = jnp.sum(coupled_ref[batch:batch + 1, :]) // per_block
+            count_ref[batch] = jnp.sum(coupled_of(batch)).astype(jnp.int32)
 
     trade.place_own(fill(), buf_ref)
     trade.await_greetings()
     trade.run(buf_ref, send_sem, recv_sem, meanwhile)
-    most = buf_ref[0, 0:1]
+    most = buf_ref[0:8, :]
     for spot in range(1, ndev):
-        most = jnp.maximum(most, buf_ref[spot, 0:1])
-    lane = lax.broadcasted_iota(jnp.int32, (1, LANES), 1)
-    most = jnp.max(jnp.where(lane == aug + 2, most, 0.0))
-    count_ref[nbatch] = most.astype(jnp.int32) // per_block
-
-
-def group_update(z, valid, x, per_block, members):
+        most = jnp.maximum(most, buf_ref[spot * trade.sent:spot * trade.sent + 8, :])
+    lane = lax.broadcasted_iota(jnp.int32, (8, LANES), 1)
+    most_ref[0] = jnp.max(jnp.where(lane == aug + 2, most, 0.0)).astype(jnp.int32)
+
+
+def group_update(z, valid, per_block, members):
     lane = lax.broadcasted_iota(jnp.int32, (GROUP, LANES), 1)
     is_member = (lane >= 1) & (lane <= members)
     z = list(z)
@@ -286,14 +304,13 @@
     for i in range(per_block):
         p = z[i]
         h = jnp.where(is_member, p, 0.0)
-        s = jnp.sum(h * h, axis=1, keepdims=True) / (members - 1)
+        s = jnp.sum(h * h, axis=1, keepdims=True) * (1.0 / (members - 1))
         y = p[:, members + 1:members + 2]
         r = p[:, members + 2:members + 3]
         q = s + r
-        c = 1.0 / ((members - 1) * q)
-        a = 1.0 / (1.0 + jnp.sqrt(r / q))
-        d = y - p[:, 0:1]
-        v = jnp.where(lane == 0, c * d, -(a * c) * h)
+        shrunk = -1.0 / ((members - 1) * (q + jnp.sqrt(q * r)))
+        d = (y - p[:, 0:1]) / ((members - 1) * q)
+        v = jnp.where(lane == 0, d, shrunk * h)
         for j in range(i + 1, per_block):
             z[j] = z[j] + v * jnp.sum(h * z[j], axis=1, keepdims=True)
         w = h
@@ -314,8 +331,6 @@
     w_half = [split2(jnp.concatenate([w[cut] for w in ws], axis=0)) for cut in cuts]
     upper = [mm3(v, w, NT) for v, w in zip(v_half, w_half)]
     across = split2(mm3(v_half[0], w_half[1], NT))
-    x_parts = split2(x)
-    seen = [mm3(x_parts, w, NT) for w in w_half]
     inverse = [
         jnp.where(row_id == col_id, 1.0, jnp.where(ahead & (differ == 1), u, 0.0)) for u in upper
     ]
@@ -324,22 +339,27 @@
         parts = [split2(i) for i in inverse]
         inner = [mm3(p, jnp.where(pairs, u, 0.0)) for p, u in zip(parts, upper)]
         inverse = [i + mm3(m, p) for i, m, p in zip(inverse, inner, parts)]
-    first = split2(mm3(seen[0], inverse[0]))
-    second = mm3(seen[1] + mm3(first, across), inverse[1])
-    return x + (mm3(first, v_half[0]) + mm3(second, v_half[1]))
-
-
-def gather_rows(read, source_ref, batch, start, per_block, z_ref):
+    inverse = [split2(i) for i in inverse]
+
+    def apply(x):
+        parts = split2(x)
+        first = split2(mm3(mm3(parts, w_half[0], NT), inverse[0]))
+        second = mm3(mm3(parts, w_half[1], NT) + mm3(first, across), inverse[1])
+        return x + (mm3(first, v_half[0]) + mm3(second, v_half[1]))
+
+    return apply
+
+
+def group_of(source_ref, buf_ref, z_ref, batch, total, start, per_block, members):
     @pl.loop(0, GROUP, unroll=8)
     def _(b):
         for i in range(per_block):
-            z_ref[pl.ds(i * GROUP + b, 1), :] = read(source_ref[batch, (start + b) * per_block + i])
-
-
-def group_of(z_ref, total, start, x, per_block, members):
+            row = source_ref[batch, (start + b) * per_block + i]
+            z_ref[pl.ds(i * GROUP + b, 1), :] = buf_ref[pl.ds(row, 1), :]
+
     valid = (start + lax.broadcasted_iota(jnp.int32, (GROUP, 1), 0) < total).astype(jnp.float32)
     z = [z_ref[i * GROUP:(i + 1) * GROUP, :] for i in range(per_block)]
-    return group_update(z, valid, x, per_block, members)
+    return group_update(z, valid, per_block, members)
 
 
 def update_kernel(batch, per_block, members, capp, source_ref, count_ref, x_ref, buf_ref, out_ref, z_ref):
@@ -348,30 +368,27 @@
 
     @pl.loop(0, (total + GROUP - 1) // GROUP)
     def _(group):
-        start = group * GROUP
-        gather_rows(lambda row: buf_ref[pl.ds(row, 1), :], source_ref, batch, start, per_block, z_ref)
-        out_ref[...] = group_of(z_ref, total, start, out_ref[...], per_block, members)
+        apply = group_of(source_ref, buf_ref, z_ref, batch, total, group * GROUP, per_block, members)
+        out_ref[...] = apply(out_ref[...])
 
 
 def rest_kernel(digits, cap, width, per_block, members, source_ref, count_ref, x_ref, buf_ref, out_ref, z_ref, *more):
     nbatch = len(more) // 3 + 1
     trade = Exchange(digits, cap, width)
     trade.greet()
-    shift = cap.bit_length() - 1
-    x = x_ref[...]
+    x = x_ref[cap:, :]
     for batch in range(nbatch):
-        def read(row, held=buf_ref):
-            return held[row >> shift, pl.ds(row & (cap - 1), 1), :]
-
-        gather_rows(read, source_ref, batch, 0, per_block, z_ref)
-        x = group_of(z_ref, count_ref[batch], 0, x[cap:], per_block, members)
+        apply = group_of(source_ref, buf_ref, z_ref, batch, count_ref[batch], 0, per_block, members)
+        if batch + 1 == nbatch:
+            out_ref[...] = apply(x)
+            break
+        buf_ref, send_sem, recv_sem = more[3 * batch:3 * batch + 3]
+        trade.place_own(apply(x[0:cap]), buf_ref)
         if batch == 0:
             trade.await_greetings()
-        if batch + 1 < nbatch:
-            buf_ref, send_sem, recv_sem = more[3 * batch:3 * batch + 3]
-            trade.place_own(x[0:cap], buf_ref)
-            trade.run(buf_ref, send_sem, recv_sem)
-    out_ref[...] = x
+        later = []
+        trade.run(buf_ref, send_sem, recv_sem, lambda: later.append(apply(x[cap:])))
+        x = later[0]
 
 
 def final_kernel(aug, per_member, x_ref, state_ref, out_ref):
@@ -408,20 +425,21 @@
     state = ensemble.reshape(aug * per_member, LANES)
     params = pltpu.CompilerParams(vmem_limit_bytes=VMEM_LIMIT)
 
-    coupled = jnp.repeat(coupling.reshape(nbatch, nblocks), per_block, axis=1)
+    coupled = coupling.reshape(nbatch, 1, nblocks)
     base = nbatch * capp
     rows = base + -(-aug // 16) * 16
     width = aug + 3
-    buf, x, source, count = pl.pallas_call(
-        functools.partial(first_kernel, digits, cap, capp, aug, per_member, base, per_block),
+    buf, x, source, count, most = pl.pallas_call(
+        functools.partial(first_kernel, digits, capp, aug, per_member, base, per_block),
         out_shape=(
-            jax.ShapeDtypeStruct((ndev, cap, LANES), jnp.float32),
+            jax.ShapeDtypeStruct((buffer_rows(ndev, capp), LANES), jnp.float32),
             jax.ShapeDtypeStruct((rows, LANES), jnp.float32),
             jax.ShapeDtypeStruct((nbatch, nobs), jnp.int32),
-            jax.ShapeDtypeStruct((nbatch + 1,), jnp.int32),
+            jax.ShapeDtypeStruct((nbatch,), jnp.int32),
+            jax.ShapeDtypeStruct((1,), jnp.int32),
         ),
         in_specs=[vspec()] * 7,
-        out_specs=(vspec(), vspec(), vspec(), sspec()),
+        out_specs=(vspec(), vspec(), vspec(), sspec(), sspec()),
         scratch_shapes=exchange_scratch(digits),
         compiler_params=pltpu.CompilerParams(
             collective_id=0, has_side_effects=True, vmem_limit_bytes=VMEM_LIMIT
@@ -433,7 +451,7 @@
     def stepwise(x, buf, source, count):
         for batch in range(nbatch):
             if batch > 0:
-                buf = exchange(x, digits, cap, width, batch, ndev)
+                buf = exchange(x, digits, capp, width, batch, ndev)
             x = pl.pallas_call(
                 functools.partial(update_kernel, batch, per_block, members, capp),
                 out_shape=jax.ShapeDtypeStruct((rows - (batch + 1) * capp, LANES), jnp.float32),
@@ -442,13 +460,13 @@
                 scratch_shapes=[z_scratch],
                 compiler_params=params,
                 name="update",
-            )(source, count, x, buf.reshape(ndev * cap, LANES))
+            )(source, count, x, buf)
         return x
 
     def together(x, buf, source, count):
-        step_scratch = [pltpu.VMEM((ndev, cap, LANES), jnp.float32)] + exchange_scratch(digits)
+        step_scratch = [pltpu.VMEM((buffer_rows(ndev, capp), LANES), jnp.float32)] + exchange_scratch(digits)
         return pl.pallas_call(
-            functools.partial(rest_kernel, digits, cap, width, per_block, members),
+            functools.partial(rest_kernel, digits, capp, width, per_block, members),
             out_shape=jax.ShapeDtypeStruct((rows - base, LANES), jnp.float32),
             in_specs=[sspec(), sspec(), vspec(), vspec()],
             out_specs=vspec(),
@@ -459,8 +477,8 @@
             name="rest",
         )(source, count, x, buf)
 
-    if is_grid(digits) and cap == capp:
-        x = lax.cond(count[nbatch] <= GROUP, together, stepwise, x, buf, source, count)
+    if is_grid(digits):
+        x = lax.cond(most.reshape(()) <= GROUP, together, stepwise, x, buf, source, count)
     else:
         x = stepwise(x, buf, source, count)
 

time: 51 us -> 51.3 us (level)
  Pallas kernels: 45.3 us -> 46.9 us
  local copies, waits for them, and re-layouts: 4.61 us -> 3.19 us
    pallas_call x2, Pallas kernels: 44.7 us -> 46.3 us  [the longest x1 33 us: together(): pl.pallas_call(functools.partial(rest_kernel, digits, capp, width, per_bl...]
    unnamed x11 -> x12, local copies, waits for them, and re-layouts: 0.71 us -> 0.02 us
    slice x1 -> x0, local copies, waits for them, and re-layouts: 0.58 us -> none  [local(): count[nbatch] <= GROUP]
where the time goes in v6:
time: 51.3 us; the launch traced here: 51.1 us
  Pallas kernels  46.9 us (91%)
  local copies, waits for them, and re-layouts  3.19 us (6%)
  between operations  0.77 us (2%)
    pallas_call x1, Pallas kernels, together(): pl.pallas_call(functools.partial(rest_kernel, digits, capp, width, per_bl...  33 us
    pallas_call x1, Pallas kernels, local(): pl.pallas_call(functools.partial(first_kernel, digits, capp, aug, per_mem...  13.4 us
    reshape x1, local copies, waits for them, and re-layouts, local(): state = ensemble.reshape(aug * per_member, LANES)  1.79 us
    reshape x1, local copies, waits for them, and re-layouts, local(): return out.reshape(aug, levels, rows_dev, cols_dev)  1.38 us

profile of v6, /device:TPU:0, one launch (start us, length us, event | category | flops | bytes accessed | tf_op | source)
XLA Modules:
  0.0 51.1 jit_solution(8403142178213393219)
XLA Ops:
  0.0 0.0 copy-start
  0.0 0.0 copy-start.1
  0.0 0.0 copy-start.2
  0.0 0.0 copy-start.3
  0.0 0.0 copy-start.4
  0.0 0.0 copy-start.5
  0.0 1.8 %reshape.15.state_ref = f32[1620,128]{1,0:T(8,128)S(1)} reshape(f32[81,10,2,128]{3,2,1,0:T(2,128)} %param.9) | data formatting | bytes 1658880 | tf_op jit(solution)/shard_map/reshape | solution.py:425
  1.8 0.0 copy-done
  1.8 0.0 copy-done.1
  1.8 0.0 copy-done.2
  1.8 0.0 copy-done.3
  1.9 0.0 copy-done.4
  1.9 0.0 copy-done.5
  1.9 13.4 %first.1 = (f32[1024,128]{1,0:T(8,128)S(1)}, f32[192,128]{1,0:T(8,128)S(1)}, s32[3,512]{1,0:T(4,128)S(1)}, s32[3]{0:T(128)S(1)}, s32[1]{0:T(128)}) custom-call(f32[3,512]{1,0:T(4,128)S(1)} %copy-done, f32[3,512]{1,0:T(4,128)S(1)} %copy-done.1, s32[3,512]{1,0:T(4,128)S(1)} %copy-done.2, s32[3,512]{1,0:T(4,128)S(1)} %copy-done.3, s32[3,512]{1,0:T(4,128)S(1)} %copy-done.4, ...), custom_call_target="tpu_custom_call" | custom-call | tf_op jit(solution)/shard_map/first/pallas_call | solution.py:432
  15.9 33.2 %conditional.1 = (f32[96,128]{1,0:T(8,128)S(1)}) conditional(s32[]{:T(128)} %bitcast.1, (s32[3,512]{1,0:T(4,128)S(1)}, s32[3]{0:T(128)S(1)}, f32[192,128]{1,0:T(8,128)S(1)}, f32[1024,128]{1,0:T(8,128)S(1)}) %tuple.11, (s32[3,512]{1,0:T(4,128)S(1)}, s32[3]{0:T(128)S(1)}, f32[192,128]{1,0:T(8,128)S(1)}, f32[1024,128]{1,0:T(8,128)S(1)}) %tuple.11), branch_computations={%region_0.0_spmd, %region_1.0_spmd} | conditional | bytes 8 | solution.py:481
  16.1 33.0 %rest.1 = f32[96,128]{1,0:T(8,128)S(1)} custom-call(s32[3,512]{1,0:T(4,128)S(1)} %get-tuple-element.28.source_ref, s32[3]{0:T(128)S(1)} %get-tuple-element.29.count_ref, f32[192,128]{1,0:T(8,128)S(1)} %get-tuple-element.30.x_ref, f32[1024,128]{1,0:T(8,128)S(1)} %get-tuple-element.31.buf_ref), custom_call_target="tpu_custom_call" | custom-call | tf_op jit(solution)/shard_map/cond/branch_1_fun/rest/pallas_call | solution.py:468
  49.1 0.6 %final.1 = f32[1620,128]{1,0:T(8,128)S(1)} custom-call(f32[96,128]{1,0:T(8,128)S(1)} %get-tuple-element.42.x_ref, f32[1620,128]{1,0:T(8,128)S(1)} %reshape.15.state_ref), custom_call_target="tpu_custom_call" | custom-call | tf_op jit(solution)/shard_map/final/pallas_call | solution.py:485
  49.7 1.4 %reshape.16 = f32[81,10,2,128]{3,2,1,0:T(2,128)} reshape(f32[1620,128]{1,0:T(8,128)S(1)} %final.1) | data formatting | bytes 1658880 | tf_op jit(solution)/shard_map/reshape | solution.py:493
Async XLA Ops:
  0.0 1.8 %copy-start = (f32[3,512]{1,0:T(4,128)S(1)}, f32[3,512]{1,0:T(4,128)}, u32[]{:S(2)}) copy-start(f32[3,512]{1,0:T(4,128)} %values_ref.1) | copy-start | bytes 18436
  0.0 1.8 %copy-start.1 = (f32[3,512]{1,0:T(4,128)S(1)}, f32[3,512]{1,0:T(4,128)}, u32[]{:S(2)}) copy-start(f32[3,512]{1,0:T(4,128)} %errors_ref.1) | copy-start | bytes 18436
  0.0 1.8 %copy-start.2 = (s32[3,512]{1,0:T(4,128)S(1)}, s32[3,512]{1,0:T(4,128)}, u32[]{:S(2)}) copy-start(s32[3,512]{1,0:T(4,128)} %device_ref.1) | copy-start | bytes 18436
  0.0 1.8 %copy-start.3 = (s32[3,512]{1,0:T(4,128)S(1)}, s32[3,512]{1,0:T(4,128)}, u32[]{:S(2)}) copy-start(s32[3,512]{1,0:T(4,128)} %cell_ref.1) | copy-start | bytes 18436
  0.0 1.8 %copy-start.4 = (s32[3,512]{1,0:T(4,128)S(1)}, s32[3,512]{1,0:T(4,128)}, u32[]{:S(2)}) copy-start(s32[3,512]{1,0:T(4,128)} %order_ref.1) | copy-start | bytes 18436
  0.0 1.9 %copy-start.5 = (s32[3,64,1,1]{1,3,2,0:T(1,128)S(1)}, s32[3,64,1,1]{1,3,2,0:T(1,128)}, u32[]{:S(2)}) copy-start(s32[3,64,1,1]{1,3,2,0:T(1,128)} %param.15) | copy-start | bytes 2308

commit v7 on v6

--- a/solution.py
+++ b/solution.py
@@ -151,8 +151,6 @@
                     meanwhile()
                 for copy in stage:
                     copy.wait_recv()
-        for copy in sends:
-            copy.wait_send()
         if sent < self.cap:
             width = self.width
             half = (width + 1) // 2
@@ -164,13 +162,19 @@
                 at = weights[-1] * sent + spot * 8
                 buf_ref[at:at + 8, :] = jnp.where(lane < half, low, high)
 
+        def settle():
+            for copy in sends:
+                copy.wait_send()
+
+        return settle
+
 
 def exchange_kernel(digits, cap, width, x_ref, buf_ref, send_sem, recv_sem):
     trade = Exchange(digits, cap, width)
     trade.greet()
     trade.place_own(x_ref[0:cap, :], buf_ref)
     trade.await_greetings()
-    trade.run(buf_ref, send_sem, recv_sem)
+    trade.run(buf_ref, send_sem, recv_sem)()
 
 
 def exchange_scratch(digits):
@@ -288,12 +292,13 @@
 
     trade.place_own(fill(), buf_ref)
     trade.await_greetings()
-    trade.run(buf_ref, send_sem, recv_sem, meanwhile)
+    settle = trade.run(buf_ref, send_sem, recv_sem, meanwhile)
     most = buf_ref[0:8, :]
     for spot in range(1, ndev):
         most = jnp.maximum(most, buf_ref[spot * trade.sent:spot * trade.sent + 8, :])
     lane = lax.broadcasted_iota(jnp.int32, (8, LANES), 1)
     most_ref[0] = jnp.max(jnp.where(lane == aug + 2, most, 0.0)).astype(jnp.int32)
+    settle()
 
 
 def group_update(z, valid, per_block, members):
@@ -376,19 +381,20 @@
     nbatch = len(more) // 3 + 1
     trade = Exchange(digits, cap, width)
     trade.greet()
-    x = x_ref[cap:, :]
+    x = x_ref[...]
+    settles = []
     for batch in range(nbatch):
         apply = group_of(source_ref, buf_ref, z_ref, batch, count_ref[batch], 0, per_block, members)
-        if batch + 1 == nbatch:
-            out_ref[...] = apply(x)
-            break
-        buf_ref, send_sem, recv_sem = more[3 * batch:3 * batch + 3]
-        trade.place_own(apply(x[0:cap]), buf_ref)
+        x = apply(x[cap:])
         if batch == 0:
             trade.await_greetings()
-        later = []
-        trade.run(buf_ref, send_sem, recv_sem, lambda: later.append(apply(x[cap:])))
-        x = later[0]
+        if batch + 1 < nbatch:
+            buf_ref, send_sem, recv_sem = more[3 * batch:3 * batch + 3]
+            trade.place_own(x[0:cap], buf_ref)
+            settles.append(trade.run(buf_ref, send_sem, recv_sem))
+    out_ref[...] = x
+    for settle in settles:
+        settle()
 
 
 def final_kernel(aug, per_member, x_ref, state_ref, out_ref):

time: 51.3 us -> 50.7 us (0.988)
  no operation moved by 1% of the time
where the time goes in v7:
time: 50.7 us; the launch traced here: 50.5 us
  Pallas kernels  46.4 us (92%)
  local copies, waits for them, and re-layouts  3.19 us (6%)
  between operations  0.77 us (2%)
    pallas_call x1, Pallas kernels, together(): pl.pallas_call(functools.partial(rest_kernel, digits, capp, width, per_bl...  32.5 us
    pallas_call x1, Pallas kernels, local(): pl.pallas_call(functools.partial(first_kernel, digits, capp, aug, per_mem...  13.3 us
    reshape x1, local copies, waits for them, and re-layouts, local(): state = ensemble.reshape(aug * per_member, LANES)  1.79 us
    reshape x1, local copies, waits for them, and re-layouts, local(): return out.reshape(aug, levels, rows_dev, cols_dev)  1.38 us

profile of v7, /device:TPU:0, one launch (start us, length us, event | category | flops | bytes accessed | tf_op | source)
XLA Modules:
  0.0 50.5 jit_solution(4575603233493682129)
XLA Ops:
  0.0 0.0 copy-start
  0.0 0.0 copy-start.1
  0.0 0.0 copy-start.2
  0.0 0.0 copy-start.3
  0.0 0.0 copy-start.4
  0.0 0.0 copy-start.5
  0.0 1.8 %reshape.15.state_ref = f32[1620,128]{1,0:T(8,128)S(1)} reshape(f32[81,10,2,128]{3,2,1,0:T(2,128)} %param.9) | data formatting | bytes 1658880 | tf_op jit(solution)/shard_map/reshape | solution.py:431
  1.8 0.0 copy-done
  1.8 0.0 copy-done.1
  1.8 0.0 copy-done.2
  1.8 0.0 copy-done.3
  1.9 0.0 copy-done.4
  1.9 0.0 copy-done.5
  1.9 13.3 %first.1 = (f32[1024,128]{1,0:T(8,128)S(1)}, f32[192,128]{1,0:T(8,128)S(1)}, s32[3,512]{1,0:T(4,128)S(1)}, s32[3]{0:T(128)S(1)}, s32[1]{0:T(128)}) custom-call(f32[3,512]{1,0:T(4,128)S(1)} %copy-done, f32[3,512]{1,0:T(4,128)S(1)} %copy-done.1, s32[3,512]{1,0:T(4,128)S(1)} %copy-done.2, s32[3,512]{1,0:T(4,128)S(1)} %copy-done.3, s32[3,512]{1,0:T(4,128)S(1)} %copy-done.4, ...), custom_call_target="tpu_custom_call" | custom-call | tf_op jit(solution)/shard_map/first/pallas_call | solution.py:438
  15.9 32.7 %conditional.1 = (f32[96,128]{1,0:T(8,128)S(1)}) conditional(s32[]{:T(128)} %bitcast.1, (s32[3,512]{1,0:T(4,128)S(1)}, s32[3]{0:T(128)S(1)}, f32[192,128]{1,0:T(8,128)S(1)}, f32[1024,128]{1,0:T(8,128)S(1)}) %tuple.11, (s32[3,512]{1,0:T(4,128)S(1)}, s32[3]{0:T(128)S(1)}, f32[192,128]{1,0:T(8,128)S(1)}, f32[1024,128]{1,0:T(8,128)S(1)}) %tuple.11), branch_computations={%region_0.0_spmd, %region_1.0_spmd} | conditional | bytes 8 | solution.py:487
  16.1 32.5 %rest.1 = f32[96,128]{1,0:T(8,128)S(1)} custom-call(s32[3,512]{1,0:T(4,128)S(1)} %get-tuple-element.28.source_ref, s32[3]{0:T(128)S(1)} %get-tuple-element.29.count_ref, f32[192,128]{1,0:T(8,128)S(1)} %get-tuple-element.30.x_ref, f32[1024,128]{1,0:T(8,128)S(1)} %get-tuple-element.31.buf_ref), custom_call_target="tpu_custom_call" | custom-call | tf_op jit(solution)/shard_map/cond/branch_1_fun/rest/pallas_call | solution.py:474
  48.5 0.6 %final.1 = f32[1620,128]{1,0:T(8,128)S(1)} custom-call(f32[96,128]{1,0:T(8,128)S(1)} %get-tuple-element.42.x_ref, f32[1620,128]{1,0:T(8,128)S(1)} %reshape.15.state_ref), custom_call_target="tpu_custom_call" | custom-call | tf_op jit(solution)/shard_map/final/pallas_call | solution.py:491
  49.1 1.4 %reshape.16 = f32[81,10,2,128]{3,2,1,0:T(2,128)} reshape(f32[1620,128]{1,0:T(8,128)S(1)} %final.1) | data formatting | bytes 1658880 | tf_op jit(solution)/shard_map/reshape | solution.py:499
Async XLA Ops:
  0.0 1.8 %copy-start = (f32[3,512]{1,0:T(4,128)S(1)}, f32[3,512]{1,0:T(4,128)}, u32[]{:S(2)}) copy-start(f32[3,512]{1,0:T(4,128)} %values_ref.1) | copy-start | bytes 18436
  0.0 1.8 %copy-start.1 = (f32[3,512]{1,0:T(4,128)S(1)}, f32[3,512]{1,0:T(4,128)}, u32[]{:S(2)}) copy-start(f32[3,512]{1,0:T(4,128)} %errors_ref.1) | copy-start | bytes 18436
  0.0 1.8 %copy-start.2 = (s32[3,512]{1,0:T(4,128)S(1)}, s32[3,512]{1,0:T(4,128)}, u32[]{:S(2)}) copy-start(s32[3,512]{1,0:T(4,128)} %device_ref.1) | copy-start | bytes 18436
  0.0 1.8 %copy-start.3 = (s32[3,512]{1,0:T(4,128)S(1)}, s32[3,512]{1,0:T(4,128)}, u32[]{:S(2)}) copy-start(s32[3,512]{1,0:T(4,128)} %cell_ref.1) | copy-start | bytes 18436
  0.0 1.8 %copy-start.4 = (s32[3,512]{1,0:T(4,128)S(1)}, s32[3,512]{1,0:T(4,128)}, u32[]{:S(2)}) copy-start(s32[3,512]{1,0:T(4,128)} %order_ref.1) | copy-start | bytes 18436
  0.0 1.9 %copy-start.5 = (s32[3,64,1,1]{1,3,2,0:T(1,128)S(1)}, s32[3,64,1,1]{1,3,2,0:T(1,128)}, u32[]{:S(2)}) copy-start(s32[3,64,1,1]{1,3,2,0:T(1,128)} %param.15) | copy-start | bytes 2308

commit v8 on v7

--- a/solution.py
+++ b/solution.py
@@ -301,7 +301,7 @@
     settle()
 
 
-def group_update(z, valid, per_block, members):
+def group_update(z, valid, x, per_block, members):
     lane = lax.broadcasted_iota(jnp.int32, (GROUP, LANES), 1)
     is_member = (lane >= 1) & (lane <= members)
     z = list(z)
@@ -335,27 +335,30 @@
     v_half = [split2(jnp.concatenate([v[cut] for v in vs], axis=0)) for cut in cuts]
     w_half = [split2(jnp.concatenate([w[cut] for w in ws], axis=0)) for cut in cuts]
     upper = [mm3(v, w, NT) for v, w in zip(v_half, w_half)]
-    across = split2(mm3(v_half[0], w_half[1], NT))
     inverse = [
         jnp.where(row_id == col_id, 1.0, jnp.where(ahead & (differ == 1), u, 0.0)) for u in upper
     ]
+    x_parts = split2(x)
+    asides = [
+        lambda: mm3(x_parts, w_half[0], NT), lambda: mm3(x_parts, w_half[1], NT),
+        lambda: split2(mm3(v_half[0], w_half[1], NT)),
+    ]
+    done = []
     for level in range(1, levels):
         pairs = ahead & (differ >= (1 << level)) & (differ < (2 << level))
         parts = [split2(i) for i in inverse]
         inner = [mm3(p, jnp.where(pairs, u, 0.0)) for p, u in zip(parts, upper)]
+        if len(done) < len(asides):
+            done.append(asides[len(done)]())
         inverse = [i + mm3(m, p) for i, m, p in zip(inverse, inner, parts)]
-    inverse = [split2(i) for i in inverse]
-
-    def apply(x):
-        parts = split2(x)
-        first = split2(mm3(mm3(parts, w_half[0], NT), inverse[0]))
-        second = mm3(mm3(parts, w_half[1], NT) + mm3(first, across), inverse[1])
-        return x + (mm3(first, v_half[0]) + mm3(second, v_half[1]))
-
-    return apply
-
-
-def group_of(source_ref, buf_ref, z_ref, batch, total, start, per_block, members):
+    done.extend(aside() for aside in asides[len(done):])
+    seen_first, seen_second, across = done
+    first = split2(mm3(seen_first, inverse[0]))
+    second = mm3(seen_second + mm3(first, across), inverse[1])
+    return x + (mm3(first, v_half[0]) + mm3(second, v_half[1]))
+
+
+def group_of(source_ref, buf_ref, z_ref, batch, total, start, x, per_block, members):
     @pl.loop(0, GROUP, unroll=8)
     def _(b):
         for i in range(per_block):
@@ -364,7 +367,7 @@
 
     valid = (start + lax.broadcasted_iota(jnp.int32, (GROUP, 1), 0) < total).astype(jnp.float32)
     z = [z_ref[i * GROUP:(i + 1) * GROUP, :] for i in range(per_block)]
-    return group_update(z, valid, per_block, members)
+    return group_update(z, valid, x, per_block, members)
 
 
 def update_kernel(batch, per_block, members, capp, source_ref, count_ref, x_ref, buf_ref, out_ref, z_ref):
@@ -373,8 +376,9 @@
 
     @pl.loop(0, (total + GROUP - 1) // GROUP)
     def _(group):
-        apply = group_of(source_ref, buf_ref, z_ref, batch, total, group * GROUP, per_block, members)
-        out_ref[...] = apply(out_ref[...])
+        out_ref[...] = group_of(
+            source_ref, buf_ref, z_ref, batch, total, group * GROUP, out_ref[...], per_block, members
+        )
 
 
 def rest_kernel(digits, cap, width, per_block, members, source_ref, count_ref, x_ref, buf_ref, out_ref, z_ref, *more):
@@ -384,8 +388,7 @@
     x = x_ref[...]
     settles = []
     for batch in range(nbatch):
-        apply = group_of(source_ref, buf_ref, z_ref, batch, count_ref[batch], 0, per_block, members)
-        x = apply(x[cap:])
+        x = group_of(source_ref, buf_ref, z_ref, batch, count_ref[batch], 0, x[cap:], per_block, members)
         if batch == 0:
             trade.await_greetings()
         if batch + 1 < nbatch:

time: 50.7 us -> 50.2 us (level)
    pallas_call x1, Pallas kernels: 32.5 us -> 32 us  [together(): pl.pallas_call(functools.partial(rest_kernel, digits, capp, width, per_bl...]
where the time goes in v8:
time: 50.2 us; the launch traced here: 50 us
  Pallas kernels  45.9 us (91%)
  local copies, waits for them, and re-layouts  3.19 us (6%)
  between operations  0.77 us (2%)
    pallas_call x1, Pallas kernels, together(): pl.pallas_call(functools.partial(rest_kernel, digits, capp, width, per_bl...  32 us
    pallas_call x1, Pallas kernels, local(): pl.pallas_call(functools.partial(first_kernel, digits, capp, aug, per_mem...  13.3 us
    reshape x1, local copies, waits for them, and re-layouts, local(): state = ensemble.reshape(aug * per_member, LANES)  1.79 us
    reshape x1, local copies, waits for them, and re-layouts, local(): return out.reshape(aug, levels, rows_dev, cols_dev)  1.38 us

profile of v8, /device:TPU:0, one launch (start us, length us, event | category | flops | bytes accessed | tf_op | source)
XLA Modules:
  0.0 50.0 jit_solution(8012526946455117758)
XLA Ops:
  0.0 0.0 copy-start
  0.0 0.0 copy-start.1
  0.0 0.0 copy-start.2
  0.0 0.0 copy-start.3
  0.0 0.0 copy-start.4
  0.0 0.0 copy-start.5
  0.0 1.8 %reshape.15.state_ref = f32[1620,128]{1,0:T(8,128)S(1)} reshape(f32[81,10,2,128]{3,2,1,0:T(2,128)} %param.9) | data formatting | bytes 1658880 | tf_op jit(solution)/shard_map/reshape | solution.py:434
  1.8 0.0 copy-done
  1.8 0.0 copy-done.1
  1.8 0.0 copy-done.2
  1.8 0.0 copy-done.3
  1.9 0.0 copy-done.4
  1.9 0.0 copy-done.5
  1.9 13.3 %first.1 = (f32[1024,128]{1,0:T(8,128)S(1)}, f32[192,128]{1,0:T(8,128)S(1)}, s32[3,512]{1,0:T(4,128)S(1)}, s32[3]{0:T(128)S(1)}, s32[1]{0:T(128)}) custom-call(f32[3,512]{1,0:T(4,128)S(1)} %copy-done, f32[3,512]{1,0:T(4,128)S(1)} %copy-done.1, s32[3,512]{1,0:T(4,128)S(1)} %copy-done.2, s32[3,512]{1,0:T(4,128)S(1)} %copy-done.3, s32[3,512]{1,0:T(4,128)S(1)} %copy-done.4, ...), custom_call_target="tpu_custom_call" | custom-call | tf_op jit(solution)/shard_map/first/pallas_call | solution.py:441
  15.9 32.2 %conditional.1 = (f32[96,128]{1,0:T(8,128)S(1)}) conditional(s32[]{:T(128)} %bitcast.1, (s32[3,512]{1,0:T(4,128)S(1)}, s32[3]{0:T(128)S(1)}, f32[192,128]{1,0:T(8,128)S(1)}, f32[1024,128]{1,0:T(8,128)S(1)}) %tuple.11, (s32[3,512]{1,0:T(4,128)S(1)}, s32[3]{0:T(128)S(1)}, f32[192,128]{1,0:T(8,128)S(1)}, f32[1024,128]{1,0:T(8,128)S(1)}) %tuple.11), branch_computations={%region_0.0_spmd, %region_1.0_spmd} | conditional | bytes 8 | solution.py:490
  16.1 32.0 %rest.1 = f32[96,128]{1,0:T(8,128)S(1)} custom-call(s32[3,512]{1,0:T(4,128)S(1)} %get-tuple-element.28.source_ref, s32[3]{0:T(128)S(1)} %get-tuple-element.29.count_ref, f32[192,128]{1,0:T(8,128)S(1)} %get-tuple-element.30.x_ref, f32[1024,128]{1,0:T(8,128)S(1)} %get-tuple-element.31.buf_ref), custom_call_target="tpu_custom_call" | custom-call | tf_op jit(solution)/shard_map/cond/branch_1_fun/rest/pallas_call | solution.py:477
  48.0 0.6 %final.1 = f32[1620,128]{1,0:T(8,128)S(1)} custom-call(f32[96,128]{1,0:T(8,128)S(1)} %get-tuple-element.42.x_ref, f32[1620,128]{1,0:T(8,128)S(1)} %reshape.15.state_ref), custom_call_target="tpu_custom_call" | custom-call | tf_op jit(solution)/shard_map/final/pallas_call | solution.py:494
  48.6 1.4 %reshape.16 = f32[81,10,2,128]{3,2,1,0:T(2,128)} reshape(f32[1620,128]{1,0:T(8,128)S(1)} %final.1) | data formatting | bytes 1658880 | tf_op jit(solution)/shard_map/reshape | solution.py:502
Async XLA Ops:
  0.0 1.8 %copy-start = (f32[3,512]{1,0:T(4,128)S(1)}, f32[3,512]{1,0:T(4,128)}, u32[]{:S(2)}) copy-start(f32[3,512]{1,0:T(4,128)} %values_ref.1) | copy-start | bytes 18436
  0.0 1.8 %copy-start.1 = (f32[3,512]{1,0:T(4,128)S(1)}, f32[3,512]{1,0:T(4,128)}, u32[]{:S(2)}) copy-start(f32[3,512]{1,0:T(4,128)} %errors_ref.1) | copy-start | bytes 18436
  0.0 1.8 %copy-start.2 = (s32[3,512]{1,0:T(4,128)S(1)}, s32[3,512]{1,0:T(4,128)}, u32[]{:S(2)}) copy-start(s32[3,512]{1,0:T(4,128)} %device_ref.1) | copy-start | bytes 18436
  0.0 1.8 %copy-start.3 = (s32[3,512]{1,0:T(4,128)S(1)}, s32[3,512]{1,0:T(4,128)}, u32[]{:S(2)}) copy-start(s32[3,512]{1,0:T(4,128)} %cell_ref.1) | copy-start | bytes 18436
  0.0 1.8 %copy-start.4 = (s32[3,512]{1,0:T(4,128)S(1)}, s32[3,512]{1,0:T(4,128)}, u32[]{:S(2)}) copy-start(s32[3,512]{1,0:T(4,128)} %order_ref.1) | copy-start | bytes 18436
  0.0 1.9 %copy-start.5 = (s32[3,64,1,1]{1,3,2,0:T(1,128)S(1)}, s32[3,64,1,1]{1,3,2,0:T(1,128)}, u32[]{:S(2)}) copy-start(s32[3,64,1,1]{1,3,2,0:T(1,128)} %param.15) | copy-start | bytes 2308

commit v9 on v8

--- a/solution.py
+++ b/solution.py
@@ -49,15 +49,6 @@
 
 def fold_of(cap, width):
     return 24 if cap == 32 and LANES - width >= (width + 1) // 2 else cap
-
-
-def buffer_rows(ndev, cap):
-    return ndev * cap
-
-
-def row_of(slab, slot, ndev, cap, width):
-    sent = fold_of(cap, width)
-    return jnp.where(slot < sent, slab * sent + slot, ndev * sent + slab * (cap - sent) + slot - sent)
 
 
 def is_grid(digits):
@@ -100,18 +91,17 @@
     def place_own(self, chunk, buf_ref):
         width, sent = self.width, self.sent
         half = (width + 1) // 2
-        own = sum(digit * weight for digit, weight in zip(self.mine, self.weights)) * sent
+        own = sum(digit * weight for digit, weight in zip(self.mine, self.weights))
         if sent < self.cap:
             tail = chunk[24:32]
             lane = lax.broadcasted_iota(jnp.int32, tail.shape, 1)
             low = jnp.where(lane < half, tail, 0.0)
             high = jnp.where((lane >= half) & (lane < width), tail, 0.0)
-            buf_ref[pl.ds(pl.multiple_of(own, 8), 24), :] = jnp.concatenate(
-                [chunk[0:8] + pltpu.roll(low, width, 1), chunk[8:16] + pltpu.roll(high, width - half, 1), chunk[16:24]],
-                axis=0,
-            )
+            buf_ref[own, 0:8] = chunk[0:8] + pltpu.roll(low, width, 1)
+            buf_ref[own, 8:16] = chunk[8:16] + pltpu.roll(high, width - half, 1)
+            buf_ref[own, 16:24] = chunk[16:24]
         else:
-            buf_ref[pl.ds(pl.multiple_of(own, 8), sent), :] = chunk
+            buf_ref[own] = chunk
 
     def run(self, buf_ref, send_sem, recv_sem, meanwhile=lambda: None):
         digits, mine, weights, sent = self.digits, self.mine, self.weights, self.sent
@@ -119,7 +109,7 @@
 
         def send(start, count, device):
             slot = len(sends)
-            part = buf_ref.at[pl.ds(pl.multiple_of(start * sent, 8), count * sent)]
+            part = buf_ref.at[pl.ds(start, count), pl.ds(0, sent)]
             copy = pltpu.make_async_remote_copy(
                 src_ref=part, dst_ref=part, send_sem=send_sem.at[slot], recv_sem=recv_sem.at[slot],
                 device_id=device, device_id_type=MESH,
@@ -155,12 +145,10 @@
             width = self.width
             half = (width + 1) // 2
             for spot in range(weights[-1]):
-                at = spot * sent
-                low = pltpu.roll(buf_ref[at:at + 8, :], LANES - width, 1)
-                high = pltpu.roll(buf_ref[at + 8:at + 16, :], LANES - width + half, 1)
+                low = pltpu.roll(buf_ref[spot, 0:8], LANES - width, 1)
+                high = pltpu.roll(buf_ref[spot, 8:16], LANES - width + half, 1)
                 lane = lax.broadcasted_iota(jnp.int32, low.shape, 1)
-                at = weights[-1] * sent + spot * 8
-                buf_ref[at:at + 8, :] = jnp.where(lane < half, low, high)
+                buf_ref[spot, 24:32] = jnp.where(lane < half, low, high)
 
         def settle():
             for copy in sends:
@@ -185,7 +173,7 @@
 def exchange(x, digits, cap, width, ident, ndev):
     return pl.pallas_call(
         functools.partial(exchange_kernel, digits, cap, width),
-        out_shape=jax.ShapeDtypeStruct((buffer_rows(ndev, cap), LANES), jnp.float32),
+        out_shape=jax.ShapeDtypeStruct((ndev, cap, LANES), jnp.float32),
         in_specs=[vspec()],
         out_specs=vspec(),
         scratch_shapes=exchange_scratch(digits),
@@ -275,7 +263,7 @@
             for axis, stride, size in digits:
                 slab = slab + pow2_part(place[axis], stride, size) * weight
                 weight *= size
-            pos = row_of(slab, rank.astype(jnp.int32), ndev, capp, aug + 3)
+            pos = slab * capp + rank.astype(jnp.int32)
             part = lax.broadcasted_iota(jnp.int32, (8, nobs), 0)
             parts = jnp.where(part == 0, pos & 63, jnp.where(part == 1, (pos >> 6) & 63, pos >> 12))
             parts = jnp.where(part < 3, parts, 0).astype(jnp.float32).astype(jnp.bfloat16)
@@ -293,9 +281,9 @@
     trade.place_own(fill(), buf_ref)
     trade.await_greetings()
     settle = trade.run(buf_ref, send_sem, recv_sem, meanwhile)
-    most = buf_ref[0:8, :]
+    most = buf_ref[0, 0:8]
     for spot in range(1, ndev):
-        most = jnp.maximum(most, buf_ref[spot * trade.sent:spot * trade.sent + 8, :])
+        most = jnp.maximum(most, buf_ref[spot, 0:8])
     lane = lax.broadcasted_iota(jnp.int32, (8, LANES), 1)
     most_ref[0] = jnp.max(jnp.where(lane == aug + 2, most, 0.0)).astype(jnp.int32)
     settle()
@@ -313,9 +301,10 @@
         y = p[:, members + 1:members + 2]
         r = p[:, members + 2:members + 3]
         q = s + r
-        shrunk = -1.0 / ((members - 1) * (q + jnp.sqrt(q * r)))
-        d = (y - p[:, 0:1]) / ((members - 1) * q)
-        v = jnp.where(lane == 0, d, shrunk * h)
+        c = 1.0 / ((members - 1) * q)
+        a = 1.0 / (1.0 + jnp.sqrt(r / q))
+        d = y - p[:, 0:1]
+        v = jnp.where(lane == 0, c * d, -(a * c) * h)
         for j in range(i + 1, per_block):
             z[j] = z[j] + v * jnp.sum(h * z[j], axis=1, keepdims=True)
         w = h
@@ -359,11 +348,14 @@
 
 
 def group_of(source_ref, buf_ref, z_ref, batch, total, start, x, per_block, members):
+    cap = buf_ref.shape[1]
+    shift = cap.bit_length() - 1
+
     @pl.loop(0, GROUP, unroll=8)
     def _(b):
         for i in range(per_block):
             row = source_ref[batch, (start + b) * per_block + i]
-            z_ref[pl.ds(i * GROUP + b, 1), :] = buf_ref[pl.ds(row, 1), :]
+            z_ref[pl.ds(i * GROUP + b, 1), :] = buf_ref[row >> shift, pl.ds(row & (cap - 1), 1), :]
 
     valid = (start + lax.broadcasted_iota(jnp.int32, (GROUP, 1), 0) < total).astype(jnp.float32)
     z = [z_ref[i * GROUP:(i + 1) * GROUP, :] for i in range(per_block)]
@@ -441,7 +433,7 @@
     buf, x, source, count, most = pl.pallas_call(
         functools.partial(first_kernel, digits, capp, aug, per_member, base, per_block),
         out_shape=(
-            jax.ShapeDtypeStruct((buffer_rows(ndev, capp), LANES), jnp.float32),
+            jax.ShapeDtypeStruct((ndev, capp, LANES), jnp.float32),
             jax.ShapeDtypeStruct((rows, LANES), jnp.float32),
             jax.ShapeDtypeStruct((nbatch, nobs), jnp.int32),
             jax.ShapeDtypeStruct((nbatch,), jnp.int32),
@@ -473,7 +465,7 @@
         return x
 
     def together(x, buf, source, count):
-        step_scratch = [pltpu.VMEM((buffer_rows(ndev, capp), LANES), jnp.float32)] + exchange_scratch(digits)
+        step_scratch = [pltpu.VMEM((ndev, capp, LANES), jnp.float32)] + exchange_scratch(digits)
         return pl.pallas_call(
             functools.partial(rest_kernel, digits, capp, width, per_block, members),
             out_shape=jax.ShapeDtypeStruct((rows - base, LANES), jnp.float32),

time: 50.2 us -> 49.6 us (0.988)
  Pallas kernels: 45.9 us -> 45.3 us
    pallas_call x1, Pallas kernels: 32 us -> 31.4 us  [together(): pl.pallas_call(functools.partial(rest_kernel, digits, capp, width, per_bl...]
where the time goes in v9:
time: 49.6 us; the launch traced here: 49.5 us
  Pallas kernels  45.3 us (91%)
  local copies, waits for them, and re-layouts  3.19 us (6%)
  between operations  0.77 us (2%)
    pallas_call x1, Pallas kernels, together(): pl.pallas_call(functools.partial(rest_kernel, digits, capp, width, per_bl...  31.4 us
    pallas_call x1, Pallas kernels, local(): pl.pallas_call(functools.partial(first_kernel, digits, capp, aug, per_mem...  13.3 us
    reshape x1, local copies, waits for them, and re-layouts, local(): state = ensemble.reshape(aug * per_member, LANES)  1.79 us
    reshape x1, local copies, waits for them, and re-layouts, local(): return out.reshape(aug, levels, rows_dev, cols_dev)  1.38 us

profile of v9, /device:TPU:0, one launch (start us, length us, event | category | flops | bytes accessed | tf_op | source)
XLA Modules:
  0.0 49.5 jit_solution(6703367442526298651)
XLA Ops:
  0.0 0.0 copy-start
  0.0 0.0 copy-start.1
  0.0 0.0 copy-start.2
  0.0 0.0 copy-start.3
  0.0 0.0 copy-start.4
  0.0 0.0 copy-start.5
  0.0 1.8 %reshape.15.state_ref = f32[1620,128]{1,0:T(8,128)S(1)} reshape(f32[81,10,2,128]{3,2,1,0:T(2,128)} %param.9) | data formatting | bytes 1658880 | tf_op jit(solution)/shard_map/reshape | solution.py:426
  1.8 0.0 copy-done
  1.8 0.0 copy-done.1
  1.8 0.0 copy-done.2
  1.8 0.0 copy-done.3
  1.9 0.0 copy-done.4
  1.9 0.0 copy-done.5
  1.9 13.3 %first.1 = (f32[32,32,128]{2,1,0:T(8,128)S(1)}, f32[192,128]{1,0:T(8,128)S(1)}, s32[3,512]{1,0:T(4,128)S(1)}, s32[3]{0:T(128)S(1)}, s32[1]{0:T(128)}) custom-call(f32[3,512]{1,0:T(4,128)S(1)} %copy-done, f32[3,512]{1,0:T(4,128)S(1)} %copy-done.1, s32[3,512]{1,0:T(4,128)S(1)} %copy-done.2, s32[3,512]{1,0:T(4,128)S(1)} %copy-done.3, s32[3,512]{1,0:T(4,128)S(1)} %copy-done.4, ...), custom_call_target="tpu_custom_call" | custom-call | tf_op jit(solution)/shard_map/first/pallas_call | solution.py:433
  15.9 31.6 %conditional.1 = (f32[96,128]{1,0:T(8,128)S(1)}) conditional(s32[]{:T(128)} %bitcast.1, (s32[3,512]{1,0:T(4,128)S(1)}, s32[3]{0:T(128)S(1)}, f32[192,128]{1,0:T(8,128)S(1)}, f32[32,32,128]{2,1,0:T(8,128)S(1)}) %tuple.11, (s32[3,512]{1,0:T(4,128)S(1)}, s32[3]{0:T(128)S(1)}, f32[192,128]{1,0:T(8,128)S(1)}, f32[32,32,128]{2,1,0:T(8,128)S(1)}) %tuple.11), branch_computations={%region_0.0_spmd, %region_1.0_spmd} | conditional | bytes 8 | solution.py:482
  16.1 31.4 %rest.1 = f32[96,128]{1,0:T(8,128)S(1)} custom-call(s32[3,512]{1,0:T(4,128)S(1)} %get-tuple-element.28.source_ref, s32[3]{0:T(128)S(1)} %get-tuple-element.29.count_ref, f32[192,128]{1,0:T(8,128)S(1)} %get-tuple-element.30.x_ref, f32[32,32,128]{2,1,0:T(8,128)S(1)} %get-tuple-element.31.buf_ref), custom_call_target="tpu_custom_call" | custom-call | tf_op jit(solution)/shard_map/cond/branch_1_fun/rest/pallas_call | solution.py:469
  47.5 0.6 %final.1 = f32[1620,128]{1,0:T(8,128)S(1)} custom-call(f32[96,128]{1,0:T(8,128)S(1)} %get-tuple-element.42.x_ref, f32[1620,128]{1,0:T(8,128)S(1)} %reshape.15.state_ref), custom_call_target="tpu_custom_call" | custom-call | tf_op jit(solution)/shard_map/final/pallas_call | solution.py:486
  48.1 1.4 %reshape.16 = f32[81,10,2,128]{3,2,1,0:T(2,128)} reshape(f32[1620,128]{1,0:T(8,128)S(1)} %final.1) | data formatting | bytes 1658880 | tf_op jit(solution)/shard_map/reshape | solution.py:494
Async XLA Ops:
  0.0 1.8 %copy-start = (f32[3,512]{1,0:T(4,128)S(1)}, f32[3,512]{1,0:T(4,128)}, u32[]{:S(2)}) copy-start(f32[3,512]{1,0:T(4,128)} %values_ref.1) | copy-start | bytes 18436
  0.0 1.8 %copy-start.1 = (f32[3,512]{1,0:T(4,128)S(1)}, f32[3,512]{1,0:T(4,128)}, u32[]{:S(2)}) copy-start(f32[3,512]{1,0:T(4,128)} %errors_ref.1) | copy-start | bytes 18436
  0.0 1.8 %copy-start.2 = (s32[3,512]{1,0:T(4,128)S(1)}, s32[3,512]{1,0:T(4,128)}, u32[]{:S(2)}) copy-start(s32[3,512]{1,0:T(4,128)} %device_ref.1) | copy-start | bytes 18436
  0.0 1.8 %copy-start.3 = (s32[3,512]{1,0:T(4,128)S(1)}, s32[3,512]{1,0:T(4,128)}, u32[]{:S(2)}) copy-start(s32[3,512]{1,0:T(4,128)} %cell_ref.1) | copy-start | bytes 18436
  0.0 1.8 %copy-start.4 = (s32[3,512]{1,0:T(4,128)S(1)}, s32[3,512]{1,0:T(4,128)}, u32[]{:S(2)}) copy-start(s32[3,512]{1,0:T(4,128)} %order_ref.1) | copy-start | bytes 18436
  0.0 1.9 %copy-start.5 = (s32[3,64,1,1]{1,3,2,0:T(1,128)S(1)}, s32[3,64,1,1]{1,3,2,0:T(1,128)}, u32[]{:S(2)}) copy-start(s32[3,64,1,1]{1,3,2,0:T(1,128)} %param.15) | copy-start | bytes 2308
